TPU v7x, 256 devices: a whole 4x4x8 slice. The times are simulated.
256 devices in a mesh: seq: 64 (over y_lo, z, x), ch: 4 (over y_hi, core).
Axes of the slice: x: 4, y: 4 (y_hi: 2, y_lo: 2; y = y_hi * 2 + y_lo), z: 8, core: 2. Of those that a mesh axis runs over, the one named last changes fastest.
Arguments:
- tokens: bfloat16 [2, 4096, 1536], P(None, 'seq', 'ch'), may hold values from -6 to 6
- norm_gain: bfloat16 [1536], replicated, may hold values from 0.5 to 2
- w_query: bfloat16 [1536, 512], P(None, 'ch'), may hold values from -1.5 to 1.5
- w_key: bfloat16 [1536, 512], P(None, 'ch'), may hold values from -0.15625 to 0.15625
- w_value: bfloat16 [1536, 1536], P(None, 'ch'), may hold values from -0.15625 to 0.15625
- w_out: bfloat16 [1536, 1536], P('ch'), may hold values from -0.15625 to 0.15625
- content_bias: bfloat16 [512], P('ch'), may hold values from -5 to 5
- rel_key: bfloat16 [32, 512], P(None, 'ch'), may hold values from -5 to 5
- rel_value: bfloat16 [32, 1536], P(None, 'ch'), may hold values from -5 to 5
- bucket_of: int32 [383], replicated, may hold values from 0 to 31, never falling along the last dimension, each value on 1 to 24 neighbouring positions
Outputs:
- mixed: bfloat16 [2, 4096, 1536], P(None, 'seq', 'ch')
Inputs may be any that keep to these rules, and one draw needn't show every extreme that they name: `bucket_of`: never falls along its dimension; every bucket covers 1 to 24 consecutive distances, and one covers the most.
All inputs are finite; a program needn't handle non-finite values.
Results may differ from a plain program's by a relative error of at most 0.015.
The roundings to bfloat16 on the way count: a program that leaves them out, or rounds other values in their place, can miss the bound.
Values may be sent and summed in bfloat16 or wider, within the bound.
No kernel may reach another device: no remote copies, remote signals or barrier semaphores. Data moves between devices by JAX's collectives and lax.ppermute only.
A program may use at most 64 MiB of HBM per device.

v0:
```python
import jax
import jax.numpy as jnp
from jax import lax
from jax.sharding import PartitionSpec as P

KEY = 64
VAL = 192
REACH = 2


eps = 1e-05


def from_behind(value, axis, steps):
    count = lax.axis_size(axis)
    pairs = [(source, (source + steps) % count) for source in range(count)]
    return lax.ppermute(value, axis, pairs)


def normalize(rows, norm_gain):
    values = rows.astype(jnp.float32)
    center = jnp.mean(values, axis=-1, keepdims=True)
    spread = jnp.mean(jnp.square(values - center), axis=-1, keepdims=True)
    return ((values - center) * lax.rsqrt(spread + eps) * norm_gain.astype(jnp.float32)).astype(
        jnp.bfloat16
    )


def project(normed, weight):
    return jnp.einsum("std,de->ste", normed, weight, preferred_element_type=jnp.float32).astype(
        jnp.bfloat16
    )


def to_window(table, block_rows, window_rows):
    lead = table.shape[:-2]
    span = table.shape[-1]
    flat = table.reshape(lead + (block_rows * span,))
    moved = flat[..., block_rows - 1 : block_rows - 1 + block_rows * (span - 1)]
    return moved.reshape(lead + (block_rows, span - 1))[..., :window_rows]


def to_distance(weights, block_rows, span):
    lead = weights.shape[:-2]
    window_rows = weights.shape[-1]
    widths = [(0, 0)] * len(lead) + [(0, 0), (0, span - 1 - window_rows)]
    padded = jnp.pad(weights, widths)
    flat = padded.reshape(lead + (block_rows * (span - 1),))
    flat = jnp.pad(flat, [(0, 0)] * len(lead) + [(block_rows - 1, 1)])
    return flat.reshape(lead + (block_rows, span))


def attend(query, keys, values, content_bias, rel_key, rel_value, bucket_of):
    sequences, block_rows, _ = query.shape
    window_rows = keys.shape[1]
    span = bucket_of.shape[0]
    buckets = rel_key.shape[0]
    heads = content_bias.shape[0] // KEY
    onehot = (bucket_of[:, None] == jnp.arange(buckets, dtype=jnp.int32)[None, :]).astype(
        jnp.bfloat16
    )
    key_dist = jnp.dot(onehot, rel_key, preferred_element_type=jnp.float32).astype(jnp.bfloat16)
    query_heads = query.reshape(sequences, block_rows, heads, KEY)
    key_heads = keys.reshape(sequences, window_rows, heads, KEY)
    value_heads = values.reshape(sequences, window_rows, heads, VAL)
    bias_heads = content_bias.reshape(heads, KEY)
    dist_heads = key_dist.reshape(span, heads, KEY)
    value_table = rel_value.reshape(-1, heads, VAL)
    content = jnp.einsum(
        "sihk,schk->shic", query_heads, key_heads, preferred_element_type=jnp.float32
    )
    biased = jnp.einsum("schk,hk->shc", key_heads, bias_heads, preferred_element_type=jnp.float32)
    by_dist = jnp.einsum(
        "sihk,dhk->shid", query_heads, dist_heads, preferred_element_type=jnp.float32
    )
    position = to_window(by_dist, block_rows, window_rows)
    scores = (content + biased[:, :, None, :] + position) * KEY ** (-0.5)
    top = jnp.max(scores, axis=-1, keepdims=True)
    expo = jnp.exp(scores - top)
    total = jnp.sum(expo, axis=-1)
    weights = expo.astype(jnp.bfloat16)
    spread_weights = to_distance(weights, block_rows, span)
    bucketed = jnp.einsum(
        "shid,db->shib", spread_weights, onehot, preferred_element_type=jnp.float32
    ).astype(jnp.bfloat16)
    summed = jnp.einsum("shic,schv->sihv", weights, value_heads, preferred_element_type=jnp.float32)
    summed = summed + jnp.einsum(
        "shib,bhv->sihv", bucketed, value_table, preferred_element_type=jnp.float32
    )
    context = summed / jnp.transpose(total, (0, 2, 1))[..., None]
    return context.astype(jnp.bfloat16).reshape(sequences, block_rows, heads * VAL)


def fetch(payload):
    arrived = {}
    for direction in (1, -1):
        carried = payload
        for step in range(REACH):
            carried = from_behind(carried, "seq", direction)
            arrived[-direction * (step + 1)] = carried
    return arrived


def body(
    tokens, norm_gain, w_query, w_key, w_value, w_out, content_bias, rel_key, rel_value, bucket_of
):
    whole = lax.all_gather(tokens, "ch", axis=2, tiled=True)
    normed = normalize(whole, norm_gain)
    query = project(normed, w_query)
    keys_here = project(normed, w_key)
    values_here = project(normed, w_value)
    key_width = keys_here.shape[2]
    packed = jnp.concatenate([keys_here, values_here], axis=2)
    arrived = fetch(packed)
    ordered = [arrived[offset] if offset != 0 else packed for offset in range(-REACH, REACH + 1)]
    window = jnp.concatenate(ordered, axis=1)
    keys = window[:, :, :key_width]
    values = window[:, :, key_width:]
    context = attend(query, keys, values, content_bias, rel_key, rel_value, bucket_of)
    partial_value = jnp.einsum(
        "sie,ed->sid", context, w_out, preferred_element_type=jnp.float32
    ).astype(jnp.bfloat16)
    summed = lax.psum_scatter(partial_value, "ch", scatter_dimension=2, tiled=True).astype(
        jnp.float32
    )
    return (tokens.astype(jnp.float32) + summed).astype(jnp.bfloat16)


def solution(mesh):
    return jax.shard_map(
        body,
        mesh=mesh,
        in_specs=(
            P(None, "seq", "ch"),
            P(),
            P(None, "ch"),
            P(None, "ch"),
            P(None, "ch"),
            P("ch", None),
            P("ch"),
            P(None, "ch"),
            P(None, "ch"),
            P(),
        ),
        out_specs=P(None, "seq", "ch"),
        check_vma=False,
    )
```

profile of v0, /device:TPU:1, one launch (start us, length us, event | category | flops | bytes accessed | tf_op | source)
XLA Modules:
  0.0 87.2 jit_solution(1491612739297413028)
XLA Ops:
  6.6 11.1 %all_gather.3 = bf16[2,64,1536]{2,1,0:T(8,128)(2,1)S(1)} all-gather(bf16[2,64,384]{2,1,0:T(8,128)(2,1)} %param.10), channel_id=1, replica_groups=mesh['seq'=64,'ch'=4] {'ch'}, dimensions={2}, use_global_device_ids=true | all-gather | bytes 491520 | tf_op jit(solution)/shard_map/all_gather | solution.py:107
  18.1 0.3 convolution_convert_fusion.4
  18.5 0.4 fusion.8
  19.0 7.1 %collective-permute-start.2 = (bf16[2,64,512]{2,1,0:T(8,128)(2,1)S(1)}, bf16[2,64,512]{2,1,0:T(8,128)(2,1)S(1)}, u32[]{:S(2)}, u32[]{:S(2)}) collective-permute-start(bf16[2,64,512]{2,1,0:T(8,128)(2,1)S(1)} %pad_maximum_fusion), channel_id=1, source_target_pairs={{0,252},{4,0},{8,4},{12,8},{16,12},{20,16},{24,20},{28,24},{32,28}... | collective-permute-start | bytes 393224 | tf_op jit(solution)/shard_map/ppermute | solution.py:17
  26.2 0.3 convolution_convert_fusion.3
  26.9 2.9 %collective-permute-done = bf16[2,64,512]{2,1,0:T(8,128)(2,1)S(1)} collective-permute-done((bf16[2,64,512]{2,1,0:T(8,128)(2,1)S(1)}, bf16[2,64,512]{2,1,0:T(8,128)(2,1)S(1)}, u32[]{:S(2)}, u32[]{:S(2)}) %collective-permute-start) | collective-permute-done | bytes 131104 | tf_op jit(solution)/shard_map/ppermute | solution.py:17
  30.1 0.6 reshape.55
  30.6 0.5 slice.18
  31.1 0.6 reshape.76
  31.8 5.8 %collective-permute-start.3 = (bf16[2,64,512]{2,1,0:T(8,128)(2,1)S(1)}, bf16[2,64,512]{2,1,0:T(8,128)(2,1)S(1)}, u32[]{:S(2)}, u32[]{:S(2)}) collective-permute-start(bf16[2,64,512]{2,1,0:T(8,128)(2,1)S(1)} %collective-permute-done.2), channel_id=1, source_target_pairs={{0,252},{4,0},{8,4},{12,8},{16,12},{20,16},{24,20},{28,24},{32,28}... | collective-permute-start | bytes 393224 | tf_op jit(solution)/shard_map/ppermute | solution.py:17
  37.5 0.9 %collective-permute-done.1 = bf16[2,64,512]{2,1,0:T(8,128)(2,1)S(1)} collective-permute-done((bf16[2,64,512]{2,1,0:T(8,128)(2,1)S(1)}, bf16[2,64,512]{2,1,0:T(8,128)(2,1)S(1)}, u32[]{:S(2)}, u32[]{:S(2)}) %collective-permute-start.1) | collective-permute-done | bytes 131104 | tf_op jit(solution)/shard_map/ppermute | solution.py:17
  38.5 1.0 %collective-permute-done.3 = bf16[2,64,512]{2,1,0:T(8,128)(2,1)S(1)} collective-permute-done((bf16[2,64,512]{2,1,0:T(8,128)(2,1)S(1)}, bf16[2,64,512]{2,1,0:T(8,128)(2,1)S(1)}, u32[]{:S(2)}, u32[]{:S(2)}) %collective-permute-start.3) | collective-permute-done | bytes 131104 | tf_op jit(solution)/shard_map/ppermute | solution.py:17
  39.9 0.3 fusion.34
  40.5 0.6 reshape.57
  41.1 0.3 pad.9
  41.4 0.4 reshape.73
  42.1 0.3 copy.26
  42.6 0.4 fusion.7
  43.3 0.4 convolution_convert_fusion
  43.7 0.6 copy.39
  44.3 1.1 %reshape.74 = bf16[1536,128]{1,0:T(8,128)(2,1)} reshape(bf16[1536,2,64]{2,1,0:T(2,128)(2,1)S(1)} %bitcast.63) | data formatting | bytes 786432
  45.4 33.1 %reduce-scatter.4.cloned.1.call-done = bf16[384,128]{1,0:T(8,128)(2,1)} async-done(((bf16[1536,128]{1,0:T(8,128)(2,1)}), bf16[384,128]{1,0:T(8,128)(2,1)}) %reduce-scatter.4.cloned.1.call-update) | async-done | bytes 98320
  78.5 1.0 %reshape.75 = bf16[384,2,64]{2,1,0:T(2,128)(2,1)S(1)} reshape(bf16[384,128]{1,0:T(8,128)(2,1)} %reduce-scatter.4.cloned.1.call-done) | data formatting | bytes 196608
  79.7 0.7 add_convert_fusion
  (54 shorter events, 2.9 us)
Async XLA Ops:
  6.5 36.7 %copy-start = (bf16[384,1536]{1,0:T(8,128)(2,1)S(1)}, bf16[384,1536]{1,0:T(8,128)(2,1)}, u32[]{:S(2)}) copy-start(bf16[384,1536]{1,0:T(8,128)(2,1)} %param.15) | copy-start | bytes 3538948
  6.5 11.5 %copy-start.4 = (bf16[1536]{0:T(1024)(128)(2,1)S(1)}, bf16[1536]{0:T(1024)(128)(2,1)}, u32[]{:S(2)}) copy-start(bf16[1536]{0:T(1024)(128)(2,1)} %param.11) | copy-start | bytes 9220
  6.5 11.5 %copy-start.7 = (bf16[1536,128]{1,0:T(8,128)(2,1)S(1)}, bf16[1536,128]{1,0:T(8,128)(2,1)}, u32[]{:S(2)}) copy-start(bf16[1536,128]{1,0:T(8,128)(2,1)} %param.13) | copy-start | bytes 1179652
  6.5 11.9 %copy-start.6 = (bf16[1536,384]{1,0:T(8,128)(2,1)S(1)}, bf16[1536,384]{1,0:T(8,128)(2,1)}, u32[]{:S(2)}) copy-start(bf16[1536,384]{1,0:T(8,128)(2,1)} %param.14) | copy-start | bytes 3538948
  6.5 72.0 %reduce-scatter.4.cloned.1.call-start = ((), (), s32[]{:S(2)}) async-start(), calls=%async_computation.1 | async-start | bytes 491520
  18.4 7.7 %copy-start.9 = (bf16[128]{0:T(256)(128)(2,1)S(1)}, bf16[128]{0:T(256)(128)(2,1)}, u32[]{:S(2)}) copy-start(bf16[128]{0:T(256)(128)(2,1)} %param.16) | copy-start | bytes 772
  18.4 7.8 %copy-start.8 = (bf16[1536,128]{1,0:T(8,128)(2,1)S(1)}, bf16[1536,128]{1,0:T(8,128)(2,1)}, u32[]{:S(2)}) copy-start(bf16[1536,128]{1,0:T(8,128)(2,1)} %param.12) | copy-start | bytes 1179652
  18.9 7.8 %copy-start.3 = (bf16[32,128]{1,0:T(8,128)(2,1)S(1)}, bf16[32,128]{1,0:T(8,128)(2,1)}, u32[]{:S(2)}) copy-start(bf16[32,128]{1,0:T(8,128)(2,1)} %param.17) | copy-start | bytes 24580
  18.9 7.8 %copy-start.5 = (s32[383]{0:T(512)S(1)}, s32[383]{0:T(512)}, u32[]{:S(2)}) copy-start(s32[383]{0:T(512)} %param.19) | copy-start | bytes 4600
  18.9 10.9 %collective-permute-start = (bf16[2,64,512]{2,1,0:T(8,128)(2,1)S(1)}, bf16[2,64,512]{2,1,0:T(8,128)(2,1)S(1)}, u32[]{:S(2)}, u32[]{:S(2)}) collective-permute-start(bf16[2,64,512]{2,1,0:T(8,128)(2,1)S(1)} %pad_maximum_fusion), channel_id=1, source_target_pairs={{0,4},{4,8},{8,12},{12,16},{16,20},{20,24},{24,28},{28,32},{32,36}... | collective-permute-start | bytes 393224 | tf_op jit(solution)/shard_map/ppermute | solution.py:17
  19.0 12.8 %collective-permute-start.2 = (bf16[2,64,512]{2,1,0:T(8,128)(2,1)S(1)}, bf16[2,64,512]{2,1,0:T(8,128)(2,1)S(1)}, u32[]{:S(2)}, u32[]{:S(2)}) collective-permute-start(bf16[2,64,512]{2,1,0:T(8,128)(2,1)S(1)} %pad_maximum_fusion), channel_id=1, source_target_pairs={{0,252},{4,0},{8,4},{12,8},{16,12},{20,16},{24,20},{28,24},{32,28}... | collective-permute-start | bytes 393224 | tf_op jit(solution)/shard_map/ppermute | solution.py:17
  29.9 8.6 %collective-permute-start.1 = (bf16[2,64,512]{2,1,0:T(8,128)(2,1)S(1)}, bf16[2,64,512]{2,1,0:T(8,128)(2,1)S(1)}, u32[]{:S(2)}, u32[]{:S(2)}) collective-permute-start(bf16[2,64,512]{2,1,0:T(8,128)(2,1)S(1)} %collective-permute-done), channel_id=1, source_target_pairs={{0,4},{4,8},{8,12},{12,16},{16,20},{20,24},{24,28},{28,32},{32,36}... | collective-permute-start | bytes 393224 | tf_op jit(solution)/shard_map/ppermute | solution.py:17
  30.0 1.6 %copy-start.2 = (bf16[32,384]{1,0:T(8,128)(2,1)S(1)}, bf16[32,384]{1,0:T(8,128)(2,1)}, u32[]{:S(2)}) copy-start(bf16[32,384]{1,0:T(8,128)(2,1)} %param.18) | copy-start | bytes 73732
  31.8 7.7 %collective-permute-start.3 = (bf16[2,64,512]{2,1,0:T(8,128)(2,1)S(1)}, bf16[2,64,512]{2,1,0:T(8,128)(2,1)S(1)}, u32[]{:S(2)}, u32[]{:S(2)}) collective-permute-start(bf16[2,64,512]{2,1,0:T(8,128)(2,1)S(1)} %collective-permute-done.2), channel_id=1, source_target_pairs={{0,252},{4,0},{8,4},{12,8},{16,12},{20,16},{24,20},{28,24},{32,28}... | collective-permute-start | bytes 393224 | tf_op jit(solution)/shard_map/ppermute | solution.py:17
  44.2 35.4 %copy-start.1 = (bf16[2,64,384]{2,1,0:T(8,128)(2,1)S(1)}, bf16[2,64,384]{2,1,0:T(8,128)(2,1)}, u32[]{:S(2)}) copy-start(bf16[2,64,384]{2,1,0:T(8,128)(2,1)} %param.10) | copy-start | bytes 294916
Sparse Core Ops, SparseCore 0:
  45.5 32.9 reduce-scatter.3
where the time goes:
time: 87.3 us; the launch traced here: 87.2 us
  waiting for transfers between devices  37.9 us (43%)
  between operations  13.7 us (16%)
  starting transfers between devices  13 us (15%)
  blocking collectives  11.1 us (13%)
  local copies, waits for them, and re-layouts  7.02 us (8%)
  matrix products  3.12 us (4%)
  other arithmetic  1.33 us (2%)
    unnamed x2, waiting for transfers between devices  33.1 us
    ppermute x4, starting transfers between devices, from_behind(): return lax.ppermute(value, axis, pairs)  13 us
    all_gather x1, blocking collectives, body(): whole = lax.all_gather(tokens, 'ch', axis=2, tiled=True)  11.1 us
    ppermute x4, waiting for transfers between devices, from_behind(): return lax.ppermute(value, axis, pairs)  4.79 us
    unnamed x27, local copies, waits for them, and re-layouts  2.92 us
  transfers between devices with their start and end apart: 5, of which 4 were waited for; matrix products, arithmetic and copies ran while one was open for 3% of the time, Pallas kernels for 0%

commit v1 on v0

v1 whole, which is shorter than its diff:
```python
import functools

import jax
import jax.numpy as jnp
from jax import lax
from jax.experimental import pallas as pl
from jax.experimental.pallas import tpu as pltpu
from jax.sharding import PartitionSpec as P

KEY = 64
VAL = 192
REACH = 2
BLK = 64
SPAN = 384
WINDOW = (2 * REACH + 1) * BLK
EPS = 1e-05
F32 = jnp.float32
BF16 = jnp.bfloat16

NT = (((1,), (1,)), ((), ()))
TN = (((0,), (0,)), ((), ()))
NN = (((1,), (0,)), ((), ()))


def dot(left, right, dims=NN):
    return lax.dot_general(left, right, dims, preferred_element_type=F32)


def by_head(rows):
    lane = lax.broadcasted_iota(jnp.int32, rows.shape, 1)
    zero = jnp.zeros_like(rows)
    return jnp.concatenate(
        [jnp.where(lane < KEY, rows, zero), jnp.where(lane >= KEY, rows, zero)], axis=0
    )


def one_hot(bucket_ref, buckets):
    return (
        bucket_ref[...] == lax.broadcasted_iota(jnp.int32, (buckets, bucket_ref.shape[1]), 0)
    ).astype(F32).astype(BF16)


def to_distance(weights):
    count = weights.shape[0]
    moved = jnp.concatenate(
        [
            pltpu.roll(weights[at : at + 8], BLK - 8 - at % BLK, 1) if at % BLK != BLK - 8 else weights[at : at + 8]
            for at in range(0, count, 8)
        ],
        axis=0,
    )
    rest = 7 - lax.broadcasted_iota(jnp.int32, moved.shape, 0) % 8
    for bit in (4, 2, 1):
        moved = jnp.where(rest & bit != 0, pltpu.roll(moved, bit, 1), moved)
    return moved


def project_kernel(whole_ref, gain_ref, key_ref, value_ref, normed_ref, packed_ref):
    sequences, rows, width = whole_ref.shape
    values = whole_ref[...].reshape(sequences * rows, width).astype(F32)
    center = jnp.mean(values, axis=-1, keepdims=True)
    moved = values - center
    spread = jnp.mean(jnp.square(moved), axis=-1, keepdims=True)
    normed = (moved * lax.rsqrt(spread + EPS) * gain_ref[...].astype(F32)).astype(BF16)
    normed_ref[...] = normed
    keys = dot(normed, key_ref[...]).astype(BF16)
    split = keys.shape[1]
    packed_ref[:, :, :split] = keys.reshape(sequences, rows, split)
    values_here = dot(normed, value_ref[...]).astype(BF16)
    packed_ref[:, :, split:] = values_here.reshape(sequences, rows, value_ref.shape[1])


def position_kernel(normed_ref, query_weight_ref, rel_key_ref, bucket_ref, query_ref, place_ref):
    query = dot(normed_ref[...], query_weight_ref[...]).astype(BF16)
    query_ref[...] = query
    hot = one_hot(bucket_ref, rel_key_ref.shape[0])
    by_distance = dot(rel_key_ref[...], hot, TN).astype(BF16)
    sequences = query.shape[0] // BLK
    for seq in range(sequences):
        stacked = by_head(query[seq * BLK : (seq + 1) * BLK])
        table = dot(stacked, by_distance)
        for head in range(2):
            part = table[head * BLK : (head + 1) * BLK]
            place_ref[seq, head * BLK : (head + 1) * BLK, :] = pltpu.roll(
                part, SPAN - (BLK - 1), 1, stride=1, stride_axis=0
            )


def attend_kernel(
    query_ref, place_ref, low2_ref, low1_ref, here_ref, up1_ref, up2_ref, bias_ref, rel_value_ref,
    bucket_ref, out_weight_ref, own_ref, first_ref, second_ref, third_ref,
):
    sequences = query_ref.shape[0] // BLK
    parts = (low2_ref, low1_ref, here_ref, up1_ref, up2_ref)
    wide = 2 * KEY
    hot = one_hot(bucket_ref, rel_value_ref.shape[0])
    bias = by_head(jnp.broadcast_to(bias_ref[...], (8, wide)))
    contexts = []
    for seq in range(sequences):
        stacked = by_head(query_ref[seq * BLK : (seq + 1) * BLK, :])
        keys = jnp.concatenate([part[seq, :, :wide] for part in parts], axis=0)
        values = jnp.concatenate([part[seq, :, wide:] for part in parts], axis=0)
        keys = jnp.concatenate([keys, jnp.zeros((SPAN - WINDOW, wide), BF16)], axis=0)
        values = jnp.concatenate([values, jnp.zeros((SPAN - WINDOW, 2 * VAL), BF16)], axis=0)
        content = dot(jnp.concatenate([stacked, bias], axis=0), keys, NT)
        biased = jnp.concatenate(
            [
                jnp.broadcast_to(content[2 * BLK : 2 * BLK + 1], (BLK, SPAN)),
                jnp.broadcast_to(content[2 * BLK + 8 : 2 * BLK + 9], (BLK, SPAN)),
            ],
            axis=0,
        )
        scores = (content[: 2 * BLK] + biased + place_ref[seq]) * KEY ** (-0.5)
        lane = lax.broadcasted_iota(jnp.int32, scores.shape, 1)
        scores = jnp.where(lane < WINDOW, scores, -jnp.inf)
        top = jnp.max(scores, axis=-1, keepdims=True)
        expo = jnp.exp(scores - top)
        total = jnp.sum(expo, axis=-1, keepdims=True)
        weights = expo.astype(BF16)
        rounded = weights.astype(F32)
        spread = to_distance(rounded).astype(BF16)
        bucketed = dot(spread, hot, NT).astype(BF16)
        summed = dot(weights, values) + dot(bucketed, rel_value_ref[...])
        summed = summed / total
        side = lax.broadcasted_iota(jnp.int32, (BLK, 2 * VAL), 1)
        contexts.append(jnp.where(side < VAL, summed[:BLK], summed[BLK:]).astype(BF16))
    context = jnp.concatenate(contexts, axis=0)
    me = lax.axis_index("ch")
    width = own_ref.shape[2]
    for order, target in enumerate((own_ref, first_ref, second_ref, third_ref)):
        at = pl.multiple_of((me ^ order) * width, width)
        partial_value = dot(context, out_weight_ref[:, pl.ds(at, width)]).astype(BF16)
        target[...] = partial_value.reshape(sequences, BLK, width)


def call(kernel, outs, cost):
    return pl.pallas_call(
        kernel,
        out_shape=outs,
        compiler_params=pltpu.CompilerParams(vmem_limit_bytes=16 * 1024 * 1024),
        cost_estimate=pl.CostEstimate(flops=cost, bytes_accessed=1 << 20, transcendentals=0),
    )


def shape(*dims, dtype=BF16):
    return jax.ShapeDtypeStruct(dims, dtype)


def shifted(value, axis, steps):
    count = lax.axis_size(axis)
    return lax.ppermute(value, axis, [(at, (at + steps) % count) for at in range(count)])


def crossed(value, axis, flip):
    count = lax.axis_size(axis)
    return lax.ppermute(value, axis, [(at, at ^ flip) for at in range(count)])


def body(
    tokens, norm_gain, w_query, w_key, w_value, w_out, content_bias, rel_key, rel_value, bucket_of
):
    sequences, rows, width = tokens.shape
    whole = lax.all_gather(tokens, "ch", axis=2, tiled=True)
    gain = norm_gain.reshape(1, -1)
    bias = content_bias.reshape(1, -1)
    bucket = jnp.pad(bucket_of, (0, SPAN - bucket_of.shape[0]), constant_values=-1).reshape(1, SPAN)
    packed_width = w_key.shape[1] + w_value.shape[1]
    normed, packed = call(
        project_kernel,
        [shape(sequences * rows, whole.shape[2]), shape(sequences, rows, packed_width)],
        300 << 20,
    )(whole, gain, w_key, w_value)
    up1 = shifted(packed, "seq", -1)
    low1 = shifted(packed, "seq", 1)
    up2 = shifted(packed, "seq", -2)
    low2 = shifted(packed, "seq", 2)
    query, place = call(
        position_kernel,
        [shape(sequences * rows, w_query.shape[1]), shape(sequences, 2 * BLK, SPAN, dtype=F32)],
        300 << 20,
    )(normed, w_query, rel_key, bucket)
    own, first, second, third = call(
        attend_kernel, [shape(sequences, rows, width)] * 4, 1 << 30
    )(query, place, low2, low1, packed, up1, up2, bias, rel_value, bucket, w_out)
    second = crossed(second, "ch", 2)
    third = crossed(third, "ch", 3)
    first = crossed(first, "ch", 1)
    summed = own.astype(F32) + first.astype(F32) + second.astype(F32) + third.astype(F32)
    return (tokens.astype(F32) + summed).astype(BF16)


def solution(mesh):
    return jax.shard_map(
        body,
        mesh=mesh,
        in_specs=(
            P(None, "seq", "ch"),
            P(),
            P(None, "ch"),
            P(None, "ch"),
            P(None, "ch"),
            P("ch", None),
            P("ch"),
            P(None, "ch"),
            P(None, "ch"),
            P(),
        ),
        out_specs=P(None, "seq", "ch"),
        check_vma=False,
    )
```

time: 87.3 us -> 48.1 us (0.55)
  waiting for transfers between devices: 37.9 us -> 13.9 us
  between operations: 13.7 us -> 0.07 us
  local copies, waits for them, and re-layouts: 7.02 us -> 3 us
  Pallas kernels: 0 us -> 3.47 us
  matrix products: 3.12 us -> 0 us
  starting transfers between devices: 13 us -> 15.7 us
    unnamed x2 -> x0, waiting for transfers between devices: 33.1 us -> none
    ppermute x4 -> x7, waiting for transfers between devices: 4.79 us -> 13.9 us  [the longest x4 8.2 us: shifted(): lax.ppermute(value, axis, [(at, (at + steps) % count) for at in range(cou...]
    pallas_call x0 -> x3, Pallas kernels: none -> 3.47 us  [the longest x1 2.14 us: body(): call(attend_kernel, [shape(sequences, rows, width)] * 4, 1 << 30)]
    dot_general x10 -> x0, matrix products: 2.93 us -> none  [the longest x3 1.08 us: project(): jnp.einsum('std,de->ste', normed, weight, preferred_element_type=jnp.floa...]
    ppermute x4 -> x7, starting transfers between devices: 13 us -> 15.7 us  [the longest x4 9.49 us: shifted(): lax.ppermute(value, axis, [(at, (at + steps) % count) for at in range(cou...]
    reshape x9 -> x2, local copies, waits for them, and re-layouts: 2.59 us -> 0.7 us  [the longest x1 0.69 us: body(): gain = norm_gain.reshape(1, -1)]
    slice x5 -> x0, local copies, waits for them, and re-layouts: 1.04 us -> none  [the longest x1 0.47 us: to_window(): moved = flat[..., block_rows - 1:block_rows - 1 + block_rows * (span - 1)]]
    unnamed x27 -> x18, local copies, waits for them, and re-layouts: 2.92 us -> 2.3 us
  transfers between devices with their start and end apart: 5 -> 7, of which waited for: 4 -> 5; matrix products, arithmetic and copies ran while one was open for 3% -> 0% of each run, Pallas kernels for 0% -> 1%
where the time goes in v1:
time: 48.1 us; the launch traced here: 47.9 us
  starting transfers between devices  15.7 us (33%)
  waiting for transfers between devices  13.9 us (29%)
  blocking collectives  11.1 us (23%)
  Pallas kernels  3.47 us (7%)
  local copies, waits for them, and re-layouts  3 us (6%)
  other arithmetic  0.71 us (1%)
    all_gather x1, blocking collectives, body(): whole = lax.all_gather(tokens, 'ch', axis=2, tiled=True)  11.1 us
    ppermute x4, starting transfers between devices, shifted(): lax.ppermute(value, axis, [(at, (at + steps) % count) for at in range(cou...  9.49 us
    ppermute x4, waiting for transfers between devices, shifted(): lax.ppermute(value, axis, [(at, (at + steps) % count) for at in range(cou...  8.2 us
    ppermute x3, starting transfers between devices, crossed(): return lax.ppermute(value, axis, [(at, at ^ flip) for at in range(count)])  6.18 us
    ppermute x3, waiting for transfers between devices, crossed(): return lax.ppermute(value, axis, [(at, at ^ flip) for at in range(count)])  5.69 us
    unnamed x18, local copies, waits for them, and re-layouts  2.3 us
    pallas_call x1, Pallas kernels, body(): call(attend_kernel, [shape(sequences, rows, width)] * 4, 1 << 30)  2.14 us
  transfers between devices with their start and end apart: 7, of which 5 were waited for; matrix products, arithmetic and copies ran while one was open for 0% of the time, Pallas kernels for 1%

profile of v1, /device:TPU:1, one launch (start us, length us, event | category | flops | bytes accessed | tf_op | source)
XLA Modules:
  0.0 47.9 jit_solution(2417547854833018736)
XLA Ops:
  0.0 0.7 %reshape.9.gain_ref = bf16[1,1536]{1,0:T(2,128)(2,1)S(1)} reshape(bf16[1536]{0:T(1024)(128)(2,1)} %param.11) | data formatting | bytes 6144 | tf_op jit(solution)/shard_map/reshape | solution.py:164
  0.7 0.0 copy-start.5
  0.7 11.1 %all_gather.3.whole_ref = bf16[2,64,1536]{2,1,0:T(8,128)(2,1)S(1)} all-gather(bf16[2,64,384]{2,1,0:T(8,128)(2,1)} %param.10), channel_id=1, replica_groups=mesh['seq'=64,'ch'=4] {'ch'}, dimensions={2}, use_global_device_ids=true | all-gather | bytes 491520 | tf_op jit(solution)/shard_map/all_gather | solution.py:163
  11.8 1.3 %copy-done = bf16[1536,384]{1,0:T(8,128)(2,1)S(1)} copy-done((bf16[1536,384]{1,0:T(8,128)(2,1)S(1)}, bf16[1536,384]{1,0:T(8,128)(2,1)}, u32[]{:S(2)}) %copy-start) | copy-done | bytes 1179672
  13.1 1.0 %copy-done.1 = bf16[1536,128]{1,0:T(8,128)(2,1)S(1)} copy-done((bf16[1536,128]{1,0:T(8,128)(2,1)S(1)}, bf16[1536,128]{1,0:T(8,128)(2,1)}, u32[]{:S(2)}) %copy-start.1) | copy-done | bytes 393240
  14.1 0.7 %shard_map.100 = (bf16[128,1536]{1,0:T(8,128)(2,1)S(1)}, bf16[2,64,512]{2,1,0:T(8,128)(2,1)S(1)}) custom-call(bf16[2,64,1536]{2,1,0:T(8,128)(2,1)S(1)} %all_gather.3.whole_ref, bf16[1,1536]{1,0:T(2,128)(2,1)S(1)} %reshape.9.gain_ref, bf16[1536,128]{1,0:T(8,128)(2,1)S(1)} %copy-done.1, bf16[1536,384]{1,0:T(8,128)(2,1)S(1)} %copy-done), custom_call_target="tpu_custom_call" | custom-call | flops 314572800 | bytes 1048576 | tf_op jit(solution)/shard_map/pallas_call | solution.py:168
  14.8 7.4 %collective-permute-start.3 = (bf16[2,64,512]{2,1,0:T(8,128)(2,1)S(1)}, bf16[2,64,512]{2,1,0:T(8,128)(2,1)S(1)}, u32[]{:S(2)}, u32[]{:S(2)}) collective-permute-start(bf16[2,64,512]{2,1,0:T(8,128)(2,1)S(1)} %get-tuple-element.16.here_ref), channel_id=1, source_target_pairs={{0,248},{4,252},{8,0},{12,4},{16,8},{20,12},{24,16},{28,20},{32,24... | collective-permute-start | bytes 393224 | tf_op jit(solution)/shard_map/ppermute | solution.py:151
  22.2 0.9 %collective-permute-start.2 = (bf16[2,64,512]{2,1,0:T(8,128)(2,1)S(1)}, bf16[2,64,512]{2,1,0:T(8,128)(2,1)S(1)}, u32[]{:S(2)}, u32[]{:S(2)}) collective-permute-start(bf16[2,64,512]{2,1,0:T(8,128)(2,1)S(1)} %get-tuple-element.16.here_ref), channel_id=1, source_target_pairs={{0,252},{4,0},{8,4},{12,8},{16,12},{20,16},{24,20},{28,24},{32,28}... | collective-permute-start | bytes 393224 | tf_op jit(solution)/shard_map/ppermute | solution.py:151
  23.0 0.6 %collective-permute-start.1 = (bf16[2,64,512]{2,1,0:T(8,128)(2,1)S(1)}, bf16[2,64,512]{2,1,0:T(8,128)(2,1)S(1)}, u32[]{:S(2)}, u32[]{:S(2)}) collective-permute-start(bf16[2,64,512]{2,1,0:T(8,128)(2,1)S(1)} %get-tuple-element.16.here_ref), channel_id=1, source_target_pairs={{0,4},{4,8},{8,12},{12,16},{16,20},{20,24},{24,28},{28,32},{32,36}... | collective-permute-start | bytes 393224 | tf_op jit(solution)/shard_map/ppermute | solution.py:151
  23.7 0.6 %collective-permute-start = (bf16[2,64,512]{2,1,0:T(8,128)(2,1)S(1)}, bf16[2,64,512]{2,1,0:T(8,128)(2,1)S(1)}, u32[]{:S(2)}, u32[]{:S(2)}) collective-permute-start(bf16[2,64,512]{2,1,0:T(8,128)(2,1)S(1)} %get-tuple-element.16.here_ref), channel_id=1, source_target_pairs={{0,8},{4,12},{8,16},{12,20},{16,24},{20,28},{24,32},{28,36},{32,40... | collective-permute-start | bytes 393224 | tf_op jit(solution)/shard_map/ppermute | solution.py:151
  24.3 0.6 %shard_map.101 = (bf16[128,128]{1,0:T(8,128)(2,1)S(1)}, f32[2,128,384]{2,1,0:T(8,128)S(1)}) custom-call(bf16[128,1536]{1,0:T(8,128)(2,1)S(1)} %get-tuple-element.13.normed_ref, bf16[1536,128]{1,0:T(8,128)(2,1)S(1)} %copy-done.3, bf16[32,128]{1,0:T(8,128)(2,1)S(1)} %copy-done.5, s32[1,384]{1,0:T(1,128)S(1)} %reshape.10.bucket_ref), custom_call_target="tpu_custom_call" | custom-call | flops 314572800 | bytes 1048576 | tf_op jit(solution)/shard_map/pallas_call | solution.py:177
  24.9 0.0 collective-permute-done.3.up2_ref
  24.9 2.9 %collective-permute-done.2.up1_ref = bf16[2,64,512]{2,1,0:T(8,128)(2,1)S(1)} collective-permute-done((bf16[2,64,512]{2,1,0:T(8,128)(2,1)S(1)}, bf16[2,64,512]{2,1,0:T(8,128)(2,1)S(1)}, u32[]{:S(2)}, u32[]{:S(2)}) %collective-permute-start.2) | collective-permute-done | bytes 131104 | tf_op jit(solution)/shard_map/ppermute | solution.py:151
  27.8 4.1 %collective-permute-done.1.low1_ref = bf16[2,64,512]{2,1,0:T(8,128)(2,1)S(1)} collective-permute-done((bf16[2,64,512]{2,1,0:T(8,128)(2,1)S(1)}, bf16[2,64,512]{2,1,0:T(8,128)(2,1)S(1)}, u32[]{:S(2)}, u32[]{:S(2)}) %collective-permute-start.1) | collective-permute-done | bytes 131104 | tf_op jit(solution)/shard_map/ppermute | solution.py:151
  31.9 1.2 %collective-permute-done.low2_ref = bf16[2,64,512]{2,1,0:T(8,128)(2,1)S(1)} collective-permute-done((bf16[2,64,512]{2,1,0:T(8,128)(2,1)S(1)}, bf16[2,64,512]{2,1,0:T(8,128)(2,1)S(1)}, u32[]{:S(2)}, u32[]{:S(2)}) %collective-permute-start) | collective-permute-done | bytes 131104 | tf_op jit(solution)/shard_map/ppermute | solution.py:151
  33.1 0.0 copy-start.7
  33.1 2.1 %shard_map.102 = (bf16[2,64,384]{2,1,0:T(8,128)(2,1)S(1)}, bf16[2,64,384]{2,1,0:T(8,128)(2,1)S(1)}, bf16[2,64,384]{2,1,0:T(8,128)(2,1)S(1)}, bf16[2,64,384]{2,1,0:T(8,128)(2,1)S(1)}) custom-call(bf16[128,128]{1,0:T(8,128)(2,1)S(1)} %get-tuple-element.14.query_ref, f32[2,128,384]{2,1,0:T(8,128)S(1)} %get-tuple-element.15.place_ref, ...), custom_call_target="tpu_custom_call" | custom-call | flops 1073741824 | bytes 1048576 | tf_op jit(solution)/shard_map/pallas_call | solution.py:182
  35.3 2.9 %collective-permute-start.4 = (bf16[2,64,384]{2,1,0:T(8,128)(2,1)S(1)}, bf16[2,64,384]{2,1,0:T(8,128)(2,1)S(1)}, u32[]{:S(2)}, u32[]{:S(2)}) collective-permute-start(bf16[2,64,384]{2,1,0:T(8,128)(2,1)S(1)} %get-tuple-element.18), channel_id=1, source_target_pairs={{0,1},{1,0},{2,3},{3,2},{4,5},{5,4},{6,7},{7,6},{8,9},{9,8},{10,11... | collective-permute-start | bytes 294920 | tf_op jit(solution)/shard_map/ppermute | solution.py:156
  38.2 2.7 %collective-permute-start.5 = (bf16[2,64,384]{2,1,0:T(8,128)(2,1)S(1)}, bf16[2,64,384]{2,1,0:T(8,128)(2,1)S(1)}, u32[]{:S(2)}, u32[]{:S(2)}) collective-permute-start(bf16[2,64,384]{2,1,0:T(8,128)(2,1)S(1)} %get-tuple-element.19), channel_id=1, source_target_pairs={{0,2},{1,3},{2,0},{3,1},{4,6},{5,7},{6,4},{7,5},{8,10},{9,11},{10,... | collective-permute-start | bytes 294920 | tf_op jit(solution)/shard_map/ppermute | solution.py:156
  40.9 0.6 %collective-permute-start.6 = (bf16[2,64,384]{2,1,0:T(8,128)(2,1)S(1)}, bf16[2,64,384]{2,1,0:T(8,128)(2,1)S(1)}, u32[]{:S(2)}, u32[]{:S(2)}) collective-permute-start(bf16[2,64,384]{2,1,0:T(8,128)(2,1)S(1)} %get-tuple-element.20), channel_id=1, source_target_pairs={{0,3},{1,2},{2,1},{3,0},{4,7},{5,6},{6,5},{7,4},{8,11},{9,10},{10,... | collective-permute-start | bytes 294920 | tf_op jit(solution)/shard_map/ppermute | solution.py:156
  41.5 0.0 collective-permute-done.4
  41.5 2.6 %collective-permute-done.5 = bf16[2,64,384]{2,1,0:T(8,128)(2,1)S(1)} collective-permute-done((bf16[2,64,384]{2,1,0:T(8,128)(2,1)S(1)}, bf16[2,64,384]{2,1,0:T(8,128)(2,1)S(1)}, u32[]{:S(2)}, u32[]{:S(2)}) %collective-permute-start.5) | collective-permute-done | bytes 98336 | tf_op jit(solution)/shard_map/ppermute | solution.py:156
  44.1 3.1 %collective-permute-done.6 = bf16[2,64,384]{2,1,0:T(8,128)(2,1)S(1)} collective-permute-done((bf16[2,64,384]{2,1,0:T(8,128)(2,1)S(1)}, bf16[2,64,384]{2,1,0:T(8,128)(2,1)S(1)}, u32[]{:S(2)}, u32[]{:S(2)}) %collective-permute-start.6) | collective-permute-done | bytes 98336 | tf_op jit(solution)/shard_map/ppermute | solution.py:156
  47.2 0.7 %add_convert_fusion = bf16[2,64,384]{2,1,0:T(8,128)(2,1)} fusion(bf16[2,64,384]{2,1,0:T(8,128)(2,1)S(1)} %collective-permute-done.6, bf16[2,64,384]{2,1,0:T(8,128)(2,1)S(1)} %collective-permute-done.5, bf16[2,64,384]{2,1,0:T(8,128)(2,1)S(1)} %collective-permute-done.4, bf16[2,64,384]{2,1,0:T(8,128)(2,1)S(1)} %get-tuple-element.17, ...), kind=kLoop, calls=%fused_computation | loop fusion | flops 491520 | bytes 589824 | tf_op jit(solution)/shard_map/convert_element_type | solution.py:189
  (16 shorter events, 0.0 us)
Async XLA Ops:
  0.7 23.6 %copy-start.8 = (s32[383]{0:T(512)S(1)}, s32[383]{0:T(512)}, u32[]{:S(2)}) copy-start(s32[383]{0:T(512)} %param.19) | copy-start | bytes 4600
  0.7 23.6 %copy-start.3 = (bf16[1536,128]{1,0:T(8,128)(2,1)S(1)}, bf16[1536,128]{1,0:T(8,128)(2,1)}, u32[]{:S(2)}) copy-start(bf16[1536,128]{1,0:T(8,128)(2,1)} %query_weight_ref.1) | copy-start | bytes 1179652
  0.7 23.6 %copy-start.5 = (bf16[32,128]{1,0:T(8,128)(2,1)S(1)}, bf16[32,128]{1,0:T(8,128)(2,1)}, u32[]{:S(2)}) copy-start(bf16[32,128]{1,0:T(8,128)(2,1)} %rel_key_ref.1) | copy-start | bytes 24580
  11.8 1.3 %copy-start = (bf16[1536,384]{1,0:T(8,128)(2,1)S(1)}, bf16[1536,384]{1,0:T(8,128)(2,1)}, u32[]{:S(2)}) copy-start(bf16[1536,384]{1,0:T(8,128)(2,1)} %value_ref.1) | copy-start | bytes 3538948
  13.1 1.0 %copy-start.1 = (bf16[1536,128]{1,0:T(8,128)(2,1)S(1)}, bf16[1536,128]{1,0:T(8,128)(2,1)}, u32[]{:S(2)}) copy-start(bf16[1536,128]{1,0:T(8,128)(2,1)} %key_ref.1) | copy-start | bytes 1179652
  14.1 19.1 %copy-start.2 = (bf16[384,1536]{1,0:T(8,128)(2,1)S(1)}, bf16[384,1536]{1,0:T(8,128)(2,1)}, u32[]{:S(2)}) copy-start(bf16[384,1536]{1,0:T(8,128)(2,1)} %out_weight_ref.1) | copy-start | bytes 3538948
  14.1 19.1 %copy-start.4 = (bf16[32,384]{1,0:T(8,128)(2,1)S(1)}, bf16[32,384]{1,0:T(8,128)(2,1)}, u32[]{:S(2)}) copy-start(bf16[32,384]{1,0:T(8,128)(2,1)} %rel_value_ref.1) | copy-start | bytes 73732
  14.1 19.1 %copy-start.6 = (bf16[128]{0:T(256)(128)(2,1)S(1)}, bf16[128]{0:T(256)(128)(2,1)}, u32[]{:S(2)}) copy-start(bf16[128]{0:T(256)(128)(2,1)} %param.16) | copy-start | bytes 772
  14.8 10.1 %collective-permute-start.3 = (bf16[2,64,512]{2,1,0:T(8,128)(2,1)S(1)}, bf16[2,64,512]{2,1,0:T(8,128)(2,1)S(1)}, u32[]{:S(2)}, u32[]{:S(2)}) collective-permute-start(bf16[2,64,512]{2,1,0:T(8,128)(2,1)S(1)} %get-tuple-element.16.here_ref), channel_id=1, source_target_pairs={{0,248},{4,252},{8,0},{12,4},{16,8},{20,12},{24,16},{28,20},{32,24... | collective-permute-start | bytes 393224 | tf_op jit(solution)/shard_map/ppermute | solution.py:151
  22.2 5.6 %collective-permute-start.2 = (bf16[2,64,512]{2,1,0:T(8,128)(2,1)S(1)}, bf16[2,64,512]{2,1,0:T(8,128)(2,1)S(1)}, u32[]{:S(2)}, u32[]{:S(2)}) collective-permute-start(bf16[2,64,512]{2,1,0:T(8,128)(2,1)S(1)} %get-tuple-element.16.here_ref), channel_id=1, source_target_pairs={{0,252},{4,0},{8,4},{12,8},{16,12},{20,16},{24,20},{28,24},{32,28}... | collective-permute-start | bytes 393224 | tf_op jit(solution)/shard_map/ppermute | solution.py:151
  23.0 8.9 %collective-permute-start.1 = (bf16[2,64,512]{2,1,0:T(8,128)(2,1)S(1)}, bf16[2,64,512]{2,1,0:T(8,128)(2,1)S(1)}, u32[]{:S(2)}, u32[]{:S(2)}) collective-permute-start(bf16[2,64,512]{2,1,0:T(8,128)(2,1)S(1)} %get-tuple-element.16.here_ref), channel_id=1, source_target_pairs={{0,4},{4,8},{8,12},{12,16},{16,20},{20,24},{24,28},{28,32},{32,36}... | collective-permute-start | bytes 393224 | tf_op jit(solution)/shard_map/ppermute | solution.py:151
  23.7 9.5 %collective-permute-start = (bf16[2,64,512]{2,1,0:T(8,128)(2,1)S(1)}, bf16[2,64,512]{2,1,0:T(8,128)(2,1)S(1)}, u32[]{:S(2)}, u32[]{:S(2)}) collective-permute-start(bf16[2,64,512]{2,1,0:T(8,128)(2,1)S(1)} %get-tuple-element.16.here_ref), channel_id=1, source_target_pairs={{0,8},{4,12},{8,16},{12,20},{16,24},{20,28},{24,32},{28,36},{32,40... | collective-permute-start | bytes 393224 | tf_op jit(solution)/shard_map/ppermute | solution.py:151
  33.1 14.0 %copy-start.7 = (bf16[2,64,384]{2,1,0:T(8,128)(2,1)S(1)}, bf16[2,64,384]{2,1,0:T(8,128)(2,1)}, u32[]{:S(2)}) copy-start(bf16[2,64,384]{2,1,0:T(8,128)(2,1)} %param.10) | copy-start | bytes 294916
  35.3 6.2 %collective-permute-start.4 = (bf16[2,64,384]{2,1,0:T(8,128)(2,1)S(1)}, bf16[2,64,384]{2,1,0:T(8,128)(2,1)S(1)}, u32[]{:S(2)}, u32[]{:S(2)}) collective-permute-start(bf16[2,64,384]{2,1,0:T(8,128)(2,1)S(1)} %get-tuple-element.18), channel_id=1, source_target_pairs={{0,1},{1,0},{2,3},{3,2},{4,5},{5,4},{6,7},{7,6},{8,9},{9,8},{10,11... | collective-permute-start | bytes 294920 | tf_op jit(solution)/shard_map/ppermute | solution.py:156
  38.2 5.9 %collective-permute-start.5 = (bf16[2,64,384]{2,1,0:T(8,128)(2,1)S(1)}, bf16[2,64,384]{2,1,0:T(8,128)(2,1)S(1)}, u32[]{:S(2)}, u32[]{:S(2)}) collective-permute-start(bf16[2,64,384]{2,1,0:T(8,128)(2,1)S(1)} %get-tuple-element.19), channel_id=1, source_target_pairs={{0,2},{1,3},{2,0},{3,1},{4,6},{5,7},{6,4},{7,5},{8,10},{9,11},{10,... | collective-permute-start | bytes 294920 | tf_op jit(solution)/shard_map/ppermute | solution.py:156
  40.9 6.3 %collective-permute-start.6 = (bf16[2,64,384]{2,1,0:T(8,128)(2,1)S(1)}, bf16[2,64,384]{2,1,0:T(8,128)(2,1)S(1)}, u32[]{:S(2)}, u32[]{:S(2)}) collective-permute-start(bf16[2,64,384]{2,1,0:T(8,128)(2,1)S(1)} %get-tuple-element.20), channel_id=1, source_target_pairs={{0,3},{1,2},{2,1},{3,0},{4,7},{5,6},{6,5},{7,4},{8,11},{9,10},{10,... | collective-permute-start | bytes 294920 | tf_op jit(solution)/shard_map/ppermute | solution.py:156

commit v2 on v1

--- a/solution.py
+++ b/solution.py
@@ -55,30 +55,51 @@
     return moved
 
 
-def project_kernel(whole_ref, gain_ref, key_ref, value_ref, normed_ref, packed_ref):
-    sequences, rows, width = whole_ref.shape
-    values = whole_ref[...].reshape(sequences * rows, width).astype(F32)
-    center = jnp.mean(values, axis=-1, keepdims=True)
-    moved = values - center
-    spread = jnp.mean(jnp.square(moved), axis=-1, keepdims=True)
-    normed = (moved * lax.rsqrt(spread + EPS) * gain_ref[...].astype(F32)).astype(BF16)
-    normed_ref[...] = normed
-    keys = dot(normed, key_ref[...]).astype(BF16)
-    split = keys.shape[1]
-    packed_ref[:, :, :split] = keys.reshape(sequences, rows, split)
-    values_here = dot(normed, value_ref[...]).astype(BF16)
-    packed_ref[:, :, split:] = values_here.reshape(sequences, rows, value_ref.shape[1])
-
-
-def position_kernel(normed_ref, query_weight_ref, rel_key_ref, bucket_ref, query_ref, place_ref):
-    query = dot(normed_ref[...], query_weight_ref[...]).astype(BF16)
-    query_ref[...] = query
+def project_kernel(
+    own_ref, beside_ref, across_ref, corner_ref, gain_ref, key_ref, value_ref, query_weight_ref,
+    packed_ref, query_ref,
+):
+    sequences, rows, width = own_ref.shape
+    me = lax.axis_index("ch")
+    pieces = [
+        part[...].reshape(sequences * rows, width).astype(F32)
+        for part in (own_ref, beside_ref, across_ref, corner_ref)
+    ]
+    count = len(pieces) * width
+    center = sum(jnp.sum(piece, axis=-1, keepdims=True) for piece in pieces) / count
+    pieces = [piece - center for piece in pieces]
+    spread = sum(jnp.sum(jnp.square(piece), axis=-1, keepdims=True) for piece in pieces) / count
+    scale = lax.rsqrt(spread + EPS)
+    normed = []
+    for order, piece in enumerate(pieces):
+        at = pl.multiple_of((me ^ order) * width, width)
+        gain = gain_ref[:, pl.ds(at, width)].astype(F32)
+        normed.append((piece * scale * gain).astype(BF16))
+
+    def project(weight_ref):
+        return sum(
+            dot(piece, weight_ref[pl.ds(pl.multiple_of((me ^ order) * width, width), width), :])
+            for order, piece in enumerate(normed)
+        ).astype(BF16)
+
+    split = key_ref.shape[1]
+    packed_ref[:, :, :split] = project(key_ref).reshape(sequences, rows, split)
+    packed_ref[:, :, split:] = project(value_ref).reshape(sequences, rows, value_ref.shape[1])
+    query_ref[...] = project(query_weight_ref)
+
+
+def table_kernel(rel_key_ref, bucket_ref, gain_ref, table_ref, gain_out_ref):
     hot = one_hot(bucket_ref, rel_key_ref.shape[0])
-    by_distance = dot(rel_key_ref[...], hot, TN).astype(BF16)
+    table_ref[...] = dot(rel_key_ref[...], hot, TN).astype(BF16)
+    gain_out_ref[...] = gain_ref[...]
+
+
+def position_kernel(query_ref, table_ref, place_ref):
+    query = query_ref[...]
     sequences = query.shape[0] // BLK
     for seq in range(sequences):
         stacked = by_head(query[seq * BLK : (seq + 1) * BLK])
-        table = dot(stacked, by_distance)
+        table = dot(stacked, table_ref[...])
         for head in range(2):
             part = table[head * BLK : (head + 1) * BLK]
             place_ref[seq, head * BLK : (head + 1) * BLK, :] = pltpu.roll(
@@ -87,7 +108,7 @@
 
 
 def attend_kernel(
-    query_ref, place_ref, low2_ref, low1_ref, here_ref, up1_ref, up2_ref, bias_ref, rel_value_ref,
+    query_ref, place_ref, up2_ref, up1_ref, here_ref, low1_ref, low2_ref, bias_ref, rel_value_ref,
     bucket_ref, out_weight_ref, own_ref, first_ref, second_ref, third_ref,
 ):
     sequences = query_ref.shape[0] // BLK
@@ -160,32 +181,36 @@
     tokens, norm_gain, w_query, w_key, w_value, w_out, content_bias, rel_key, rel_value, bucket_of
 ):
     sequences, rows, width = tokens.shape
-    whole = lax.all_gather(tokens, "ch", axis=2, tiled=True)
     gain = norm_gain.reshape(1, -1)
     bias = content_bias.reshape(1, -1)
     bucket = jnp.pad(bucket_of, (0, SPAN - bucket_of.shape[0]), constant_values=-1).reshape(1, SPAN)
     packed_width = w_key.shape[1] + w_value.shape[1]
-    normed, packed = call(
+    across = crossed(tokens, "ch", 2)
+    beside = crossed(tokens, "ch", 1)
+    table, gain = call(
+        table_kernel, [shape(w_key.shape[1], SPAN), shape(*gain.shape)], 20 << 30
+    )(rel_key, bucket, gain)
+    across, table, gain = lax.optimization_barrier((across, table, gain))
+    corner = crossed(across, "ch", 1)
+    packed, query = call(
         project_kernel,
-        [shape(sequences * rows, whole.shape[2]), shape(sequences, rows, packed_width)],
+        [shape(sequences, rows, packed_width), shape(sequences * rows, w_query.shape[1])],
         300 << 20,
-    )(whole, gain, w_key, w_value)
+    )(tokens, beside, across, corner, gain, w_key, w_value, w_query)
+    low2 = shifted(packed, "seq", 2)
+    low1 = shifted(packed, "seq", 1)
     up1 = shifted(packed, "seq", -1)
-    low1 = shifted(packed, "seq", 1)
     up2 = shifted(packed, "seq", -2)
-    low2 = shifted(packed, "seq", 2)
-    query, place = call(
-        position_kernel,
-        [shape(sequences * rows, w_query.shape[1]), shape(sequences, 2 * BLK, SPAN, dtype=F32)],
-        300 << 20,
-    )(normed, w_query, rel_key, bucket)
-    own, first, second, third = call(
+    place = call(
+        position_kernel, shape(sequences, 2 * BLK, SPAN, dtype=F32), 300 << 20
+    )(query, table)
+    own, beside, across, corner = call(
         attend_kernel, [shape(sequences, rows, width)] * 4, 1 << 30
-    )(query, place, low2, low1, packed, up1, up2, bias, rel_value, bucket, w_out)
-    second = crossed(second, "ch", 2)
-    third = crossed(third, "ch", 3)
-    first = crossed(first, "ch", 1)
-    summed = own.astype(F32) + first.astype(F32) + second.astype(F32) + third.astype(F32)
+    )(query, place, up2, up1, packed, low1, low2, bias, rel_value, bucket, w_out)
+    pair = (across.astype(F32) + crossed(corner, "ch", 1).astype(F32)).astype(BF16)
+    beside = crossed(beside, "ch", 1)
+    pair = crossed(pair, "ch", 2)
+    summed = own.astype(F32) + beside.astype(F32) + pair.astype(F32)
     return (tokens.astype(F32) + summed).astype(BF16)
 
 

time: 48.1 us -> 38.3 us (0.80)
  blocking collectives: 11.1 us -> 0 us
  starting transfers between devices: 15.7 us -> 19.5 us
  waiting for transfers between devices: 13.9 us -> 12.1 us
  local copies, waits for them, and re-layouts: 3 us -> 2.1 us
    all_gather x1 -> x0, blocking collectives: 11.1 us -> none  [body(): whole = lax.all_gather(tokens, 'ch', axis=2, tiled=True)]
    ppermute x3 -> x6, starting transfers between devices: 6.18 us -> 10.1 us  [crossed(): return lax.ppermute(value, axis, [(at, at ^ flip) for at in range(count)])]
    ppermute x4, waiting for transfers between devices: 8.2 us -> 5.07 us  [shifted(): lax.ppermute(value, axis, [(at, (at + steps) % count) for at in range(cou...]
    unnamed x18 -> x16, local copies, waits for them, and re-layouts: 2.3 us -> 0.72 us
    ppermute x3 -> x6, waiting for transfers between devices: 5.69 us -> 7.06 us  [crossed(): return lax.ppermute(value, axis, [(at, at ^ flip) for at in range(count)])]
    pad x1, local copies, waits for them, and re-layouts: 0.01 us -> 0.68 us  [body(): jnp.pad(bucket_of, (0, SPAN - bucket_of.shape[0]), constant_values=-1)]
    pallas_call x2 -> x3, Pallas kernels: 1.33 us -> 1.39 us  [the longest x1 0.87 us: body(): call(project_kernel, [shape(sequences, rows, packed_width), shape(sequenc...]
  transfers between devices with their start and end apart: 7 -> 10, of which waited for: 5 -> 7; matrix products, arithmetic and copies ran while one was open for 0% -> 4% of each run, Pallas kernels for 1% -> 1%
where the time goes in v2:
time: 38.3 us; the launch traced here: 38.1 us
  starting transfers between devices  19.5 us (51%)
  waiting for transfers between devices  12.1 us (32%)
  Pallas kernels  3.52 us (9%)
  local copies, waits for them, and re-layouts  2.1 us (5%)
  other arithmetic  0.72 us (2%)
    ppermute x6, starting transfers between devices, crossed(): return lax.ppermute(value, axis, [(at, at ^ flip) for at in range(count)])  10.1 us
    ppermute x4, starting transfers between devices, shifted(): lax.ppermute(value, axis, [(at, (at + steps) % count) for at in range(cou...  9.49 us
    ppermute x6, waiting for transfers between devices, crossed(): return lax.ppermute(value, axis, [(at, at ^ flip) for at in range(count)])  7.06 us
    ppermute x4, waiting for transfers between devices, shifted(): lax.ppermute(value, axis, [(at, (at + steps) % count) for at in range(cou...  5.07 us
    pallas_call x1, Pallas kernels, body(): call(attend_kernel, [shape(sequences, rows, width)] * 4, 1 << 30)  2.14 us
    pallas_call x1, Pallas kernels, body(): call(project_kernel, [shape(sequences, rows, packed_width), shape(sequenc...  0.87 us
  transfers between devices with their start and end apart: 10, of which 7 were waited for; matrix products, arithmetic and copies ran while one was open for 4% of the time, Pallas kernels for 1%

profile of v2, /device:TPU:1, one launch (start us, length us, event | category | flops | bytes accessed | tf_op | source)
XLA Modules:
  0.0 38.1 jit_solution(14374872527691093144)
XLA Ops:
  0.0 3.2 %collective-permute-start = (bf16[2,64,384]{2,1,0:T(8,128)(2,1)}, bf16[2,64,384]{2,1,0:T(8,128)(2,1)S(1)}, u32[]{:S(2)}, u32[]{:S(2)}) collective-permute-start(bf16[2,64,384]{2,1,0:T(8,128)(2,1)} %own_ref.1), channel_id=1, source_target_pairs={{0,1},{1,0},{2,3},{3,2},{4,5},{5,4},{6,7},{7,6},{8,9},{9,8},{10,11... | collective-permute-start | bytes 294920 | tf_op jit(solution)/shard_map/ppermute | solution.py:177
  3.2 1.2 %collective-permute-start.1 = (bf16[2,64,384]{2,1,0:T(8,128)(2,1)}, bf16[2,64,384]{2,1,0:T(8,128)(2,1)S(1)}, u32[]{:S(2)}, u32[]{:S(2)}) collective-permute-start(bf16[2,64,384]{2,1,0:T(8,128)(2,1)} %own_ref.1), channel_id=1, source_target_pairs={{0,2},{1,3},{2,0},{3,1},{4,6},{5,7},{6,4},{7,5},{8,10},{9,11},{10,... | collective-permute-start | bytes 294920 | tf_op jit(solution)/shard_map/ppermute | solution.py:177
  4.4 0.7 %pad.4 = s32[384]{0:T(512)S(1)} pad(s32[383]{0:T(512)} %param.19, s32[]{:T(128)} %constant.0.clone.1), padding=0_1 | pad | bytes 3072 | tf_op jit(solution)/shard_map/jit(_pad)/pad | solution.py:186
  5.1 0.7 %reshape.10.gain_ref = bf16[1,1536]{1,0:T(2,128)(2,1)S(1)} reshape(bf16[1536]{0:T(1024)(128)(2,1)} %param.11) | data formatting | bytes 6144 | tf_op jit(solution)/shard_map/reshape | solution.py:184
  5.8 0.7 %copy-done.6 = bf16[32,128]{1,0:T(8,128)(2,1)S(1)} copy-done((bf16[32,128]{1,0:T(8,128)(2,1)S(1)}, bf16[32,128]{1,0:T(8,128)(2,1)}, u32[]{:S(2)}) %copy-start.6) | copy-done | bytes 8216
  6.5 0.2 shard_map.100
  6.7 2.7 %collective-permute-done.1.across_ref = bf16[2,64,384]{2,1,0:T(8,128)(2,1)S(1)} collective-permute-done((bf16[2,64,384]{2,1,0:T(8,128)(2,1)}, bf16[2,64,384]{2,1,0:T(8,128)(2,1)S(1)}, u32[]{:S(2)}, u32[]{:S(2)}) %collective-permute-start.1) | collective-permute-done | bytes 98336 | tf_op jit(solution)/shard_map/ppermute | solution.py:177
  9.4 0.8 %collective-permute-start.2 = (bf16[2,64,384]{2,1,0:T(8,128)(2,1)S(1)}, bf16[2,64,384]{2,1,0:T(8,128)(2,1)S(1)}, u32[]{:S(2)}, u32[]{:S(2)}) collective-permute-start(bf16[2,64,384]{2,1,0:T(8,128)(2,1)S(1)} %collective-permute-done.1.across_ref), channel_id=1, source_target_pairs={{0,1},{1,0},{2,3},{3,2},{4,5},{5,4},{6,7},{7,6},{8,9},{9,8},{10,11... | collective-permute-start | bytes 294920 | tf_op jit(solution)/shard_map/ppermute | solution.py:177
  10.2 0.9 %collective-permute-done.2.corner_ref = bf16[2,64,384]{2,1,0:T(8,128)(2,1)S(1)} collective-permute-done((bf16[2,64,384]{2,1,0:T(8,128)(2,1)S(1)}, bf16[2,64,384]{2,1,0:T(8,128)(2,1)S(1)}, u32[]{:S(2)}, u32[]{:S(2)}) %collective-permute-start.2) | collective-permute-done | bytes 98336 | tf_op jit(solution)/shard_map/ppermute | solution.py:177
  11.1 0.9 %shard_map.101 = (bf16[2,64,512]{2,1,0:T(8,128)(2,1)S(1)}, bf16[128,128]{1,0:T(8,128)(2,1)S(1)}) custom-call(bf16[2,64,384]{2,1,0:T(8,128)(2,1)S(1)} %copy-done.3, bf16[2,64,384]{2,1,0:T(8,128)(2,1)S(1)} %collective-permute-done.beside_ref, bf16[2,64,384]{2,1,0:T(8,128)(2,1)S(1)} %collective-permute-done.1.across_ref, ...), custom_call_target="tpu_custom_call" | custom-call | flops 314572800 | bytes 1048576 | tf_op jit(solution)/shard_map/pallas_call | solution.py:195
  12.0 1.1 %collective-permute-start.6 = (bf16[2,64,512]{2,1,0:T(8,128)(2,1)S(1)}, bf16[2,64,512]{2,1,0:T(8,128)(2,1)S(1)}, u32[]{:S(2)}, u32[]{:S(2)}) collective-permute-start(bf16[2,64,512]{2,1,0:T(8,128)(2,1)S(1)} %get-tuple-element.22.here_ref), channel_id=1, source_target_pairs={{0,8},{4,12},{8,16},{12,20},{16,24},{20,28},{24,32},{28,36},{32,40... | collective-permute-start | bytes 393224 | tf_op jit(solution)/shard_map/ppermute | solution.py:172
  13.1 0.3 collective-permute-start.5
  13.4 5.9 %collective-permute-start.4 = (bf16[2,64,512]{2,1,0:T(8,128)(2,1)S(1)}, bf16[2,64,512]{2,1,0:T(8,128)(2,1)S(1)}, u32[]{:S(2)}, u32[]{:S(2)}) collective-permute-start(bf16[2,64,512]{2,1,0:T(8,128)(2,1)S(1)} %get-tuple-element.22.here_ref), channel_id=1, source_target_pairs={{0,252},{4,0},{8,4},{12,8},{16,12},{20,16},{24,20},{28,24},{32,28}... | collective-permute-start | bytes 393224 | tf_op jit(solution)/shard_map/ppermute | solution.py:172
  19.3 2.2 %collective-permute-start.3 = (bf16[2,64,512]{2,1,0:T(8,128)(2,1)S(1)}, bf16[2,64,512]{2,1,0:T(8,128)(2,1)S(1)}, u32[]{:S(2)}, u32[]{:S(2)}) collective-permute-start(bf16[2,64,512]{2,1,0:T(8,128)(2,1)S(1)} %get-tuple-element.22.here_ref), channel_id=1, source_target_pairs={{0,248},{4,252},{8,0},{12,4},{16,8},{20,12},{24,16},{28,20},{32,24... | collective-permute-start | bytes 393224 | tf_op jit(solution)/shard_map/ppermute | solution.py:172
  21.5 0.3 shard_map.102.place_ref
  21.8 1.2 %collective-permute-done.6.low2_ref = bf16[2,64,512]{2,1,0:T(8,128)(2,1)S(1)} collective-permute-done((bf16[2,64,512]{2,1,0:T(8,128)(2,1)S(1)}, bf16[2,64,512]{2,1,0:T(8,128)(2,1)S(1)}, u32[]{:S(2)}, u32[]{:S(2)}) %collective-permute-start.6) | collective-permute-done | bytes 131104 | tf_op jit(solution)/shard_map/ppermute | solution.py:172
  23.0 3.6 %collective-permute-done.5.low1_ref = bf16[2,64,512]{2,1,0:T(8,128)(2,1)S(1)} collective-permute-done((bf16[2,64,512]{2,1,0:T(8,128)(2,1)S(1)}, bf16[2,64,512]{2,1,0:T(8,128)(2,1)S(1)}, u32[]{:S(2)}, u32[]{:S(2)}) %collective-permute-start.5) | collective-permute-done | bytes 131104 | tf_op jit(solution)/shard_map/ppermute | solution.py:172
  26.6 0.3 collective-permute-done.3.up2_ref
  26.9 2.1 %shard_map.103 = (bf16[2,64,384]{2,1,0:T(8,128)(2,1)S(1)}, bf16[2,64,384]{2,1,0:T(8,128)(2,1)S(1)}, bf16[2,64,384]{2,1,0:T(8,128)(2,1)S(1)}, bf16[2,64,384]{2,1,0:T(8,128)(2,1)S(1)}) custom-call(bf16[128,128]{1,0:T(8,128)(2,1)S(1)} %get-tuple-element.20.query_ref, f32[2,128,384]{2,1,0:T(8,128)S(1)} %shard_map.102.place_ref, ...), custom_call_target="tpu_custom_call" | custom-call | flops 1073741824 | bytes 1048576 | tf_op jit(solution)/shard_map/pallas_call | solution.py:207
  29.0 1.7 %collective-permute-start.8 = (bf16[2,64,384]{2,1,0:T(8,128)(2,1)S(1)}, bf16[2,64,384]{2,1,0:T(8,128)(2,1)S(1)}, u32[]{:S(2)}, u32[]{:S(2)}) collective-permute-start(bf16[2,64,384]{2,1,0:T(8,128)(2,1)S(1)} %get-tuple-element.26), channel_id=1, source_target_pairs={{0,1},{1,0},{2,3},{3,2},{4,5},{5,4},{6,7},{7,6},{8,9},{9,8},{10,11... | collective-permute-start | bytes 294920 | tf_op jit(solution)/shard_map/ppermute | solution.py:177
  30.9 0.8 %collective-permute-done.8 = bf16[2,64,384]{2,1,0:T(8,128)(2,1)S(1)} collective-permute-done((bf16[2,64,384]{2,1,0:T(8,128)(2,1)S(1)}, bf16[2,64,384]{2,1,0:T(8,128)(2,1)S(1)}, u32[]{:S(2)}, u32[]{:S(2)}) %collective-permute-start.8) | collective-permute-done | bytes 98336 | tf_op jit(solution)/shard_map/ppermute | solution.py:177
  31.8 3.0 %collective-permute-start.9 = (bf16[2,64,384]{2,1,0:T(8,128)(2,1)S(1)}, bf16[2,64,384]{2,1,0:T(8,128)(2,1)S(1)}, u32[]{:S(2)}, u32[]{:S(2)}) collective-permute-start(bf16[2,64,384]{2,1,0:T(8,128)(2,1)S(1)} %add_convert_fusion.1), channel_id=1, source_target_pairs={{0,2},{1,3},{2,0},{3,1},{4,6},{5,7},{6,4},{7,5},{8,10},{9,11},{10,... | collective-permute-start | bytes 294920 | tf_op jit(solution)/shard_map/ppermute | solution.py:177
  34.8 2.6 %collective-permute-done.9 = bf16[2,64,384]{2,1,0:T(8,128)(2,1)S(1)} collective-permute-done((bf16[2,64,384]{2,1,0:T(8,128)(2,1)S(1)}, bf16[2,64,384]{2,1,0:T(8,128)(2,1)S(1)}, u32[]{:S(2)}, u32[]{:S(2)}) %collective-permute-start.9) | collective-permute-done | bytes 98336 | tf_op jit(solution)/shard_map/ppermute | solution.py:177
  37.4 0.7 %add_convert_fusion = bf16[2,64,384]{2,1,0:T(8,128)(2,1)} fusion(bf16[2,64,384]{2,1,0:T(8,128)(2,1)S(1)} %collective-permute-done.9, bf16[2,64,384]{2,1,0:T(8,128)(2,1)S(1)} %collective-permute-done.7, bf16[2,64,384]{2,1,0:T(8,128)(2,1)S(1)} %get-tuple-element.23, bf16[2,64,384]{2,1,0:T(8,128)(2,1)S(1)} %copy-done.3), kind=kLoop, calls=%fused_computation | loop fusion | flops 393216 | bytes 491520 | tf_op jit(solution)/shard_map/convert_element_type | solution.py:214
  (21 shorter events, 0.2 us)
Async XLA Ops:
  0.0 10.2 %collective-permute-start = (bf16[2,64,384]{2,1,0:T(8,128)(2,1)}, bf16[2,64,384]{2,1,0:T(8,128)(2,1)S(1)}, u32[]{:S(2)}, u32[]{:S(2)}) collective-permute-start(bf16[2,64,384]{2,1,0:T(8,128)(2,1)} %own_ref.1), channel_id=1, source_target_pairs={{0,1},{1,0},{2,3},{3,2},{4,5},{5,4},{6,7},{7,6},{8,9},{9,8},{10,11... | collective-permute-start | bytes 294920 | tf_op jit(solution)/shard_map/ppermute | solution.py:177
  3.2 6.1 %collective-permute-start.1 = (bf16[2,64,384]{2,1,0:T(8,128)(2,1)}, bf16[2,64,384]{2,1,0:T(8,128)(2,1)S(1)}, u32[]{:S(2)}, u32[]{:S(2)}) collective-permute-start(bf16[2,64,384]{2,1,0:T(8,128)(2,1)} %own_ref.1), channel_id=1, source_target_pairs={{0,2},{1,3},{2,0},{3,1},{4,6},{5,7},{6,4},{7,5},{8,10},{9,11},{10,... | collective-permute-start | bytes 294920 | tf_op jit(solution)/shard_map/ppermute | solution.py:177
  5.8 0.7 %copy-start.6 = (bf16[32,128]{1,0:T(8,128)(2,1)S(1)}, bf16[32,128]{1,0:T(8,128)(2,1)}, u32[]{:S(2)}) copy-start(bf16[32,128]{1,0:T(8,128)(2,1)} %rel_key_ref.1) | copy-start | bytes 24580
  6.5 4.6 %copy-start = (bf16[1536,384]{1,0:T(8,128)(2,1)S(1)}, bf16[1536,384]{1,0:T(8,128)(2,1)}, u32[]{:S(2)}) copy-start(bf16[1536,384]{1,0:T(8,128)(2,1)} %value_ref.1) | copy-start | bytes 3538948
  6.5 4.6 %copy-start.1 = (bf16[1536,128]{1,0:T(8,128)(2,1)S(1)}, bf16[1536,128]{1,0:T(8,128)(2,1)}, u32[]{:S(2)}) copy-start(bf16[1536,128]{1,0:T(8,128)(2,1)} %key_ref.1) | copy-start | bytes 1179652
  6.5 4.6 %copy-start.2 = (bf16[1536,128]{1,0:T(8,128)(2,1)S(1)}, bf16[1536,128]{1,0:T(8,128)(2,1)}, u32[]{:S(2)}) copy-start(bf16[1536,128]{1,0:T(8,128)(2,1)} %query_weight_ref.1) | copy-start | bytes 1179652
  6.5 4.6 %copy-start.3 = (bf16[2,64,384]{2,1,0:T(8,128)(2,1)S(1)}, bf16[2,64,384]{2,1,0:T(8,128)(2,1)}, u32[]{:S(2)}) copy-start(bf16[2,64,384]{2,1,0:T(8,128)(2,1)} %own_ref.1) | copy-start | bytes 294916
  9.4 17.5 %copy-start.4 = (bf16[384,1536]{1,0:T(8,128)(2,1)S(1)}, bf16[384,1536]{1,0:T(8,128)(2,1)}, u32[]{:S(2)}) copy-start(bf16[384,1536]{1,0:T(8,128)(2,1)} %out_weight_ref.1) | copy-start | bytes 3538948
  9.4 17.5 %copy-start.5 = (bf16[32,384]{1,0:T(8,128)(2,1)S(1)}, bf16[32,384]{1,0:T(8,128)(2,1)}, u32[]{:S(2)}) copy-start(bf16[32,384]{1,0:T(8,128)(2,1)} %rel_value_ref.1) | copy-start | bytes 73732
  9.4 17.5 %copy-start.7 = (bf16[128]{0:T(256)(128)(2,1)S(1)}, bf16[128]{0:T(256)(128)(2,1)}, u32[]{:S(2)}) copy-start(bf16[128]{0:T(256)(128)(2,1)} %param.16) | copy-start | bytes 772
  9.4 1.7 %collective-permute-start.2 = (bf16[2,64,384]{2,1,0:T(8,128)(2,1)S(1)}, bf16[2,64,384]{2,1,0:T(8,128)(2,1)S(1)}, u32[]{:S(2)}, u32[]{:S(2)}) collective-permute-start(bf16[2,64,384]{2,1,0:T(8,128)(2,1)S(1)} %collective-permute-done.1.across_ref), channel_id=1, source_target_pairs={{0,1},{1,0},{2,3},{3,2},{4,5},{5,4},{6,7},{7,6},{8,9},{9,8},{10,11... | collective-permute-start | bytes 294920 | tf_op jit(solution)/shard_map/ppermute | solution.py:177
  12.0 11.0 %collective-permute-start.6 = (bf16[2,64,512]{2,1,0:T(8,128)(2,1)S(1)}, bf16[2,64,512]{2,1,0:T(8,128)(2,1)S(1)}, u32[]{:S(2)}, u32[]{:S(2)}) collective-permute-start(bf16[2,64,512]{2,1,0:T(8,128)(2,1)S(1)} %get-tuple-element.22.here_ref), channel_id=1, source_target_pairs={{0,8},{4,12},{8,16},{12,20},{16,24},{20,28},{24,32},{28,36},{32,40... | collective-permute-start | bytes 393224 | tf_op jit(solution)/shard_map/ppermute | solution.py:172
  13.1 13.5 %collective-permute-start.5 = (bf16[2,64,512]{2,1,0:T(8,128)(2,1)S(1)}, bf16[2,64,512]{2,1,0:T(8,128)(2,1)S(1)}, u32[]{:S(2)}, u32[]{:S(2)}) collective-permute-start(bf16[2,64,512]{2,1,0:T(8,128)(2,1)S(1)} %get-tuple-element.22.here_ref), channel_id=1, source_target_pairs={{0,4},{4,8},{8,12},{12,16},{16,20},{20,24},{24,28},{28,32},{32,36}... | collective-permute-start | bytes 393224 | tf_op jit(solution)/shard_map/ppermute | solution.py:172
  13.4 13.2 %collective-permute-start.4 = (bf16[2,64,512]{2,1,0:T(8,128)(2,1)S(1)}, bf16[2,64,512]{2,1,0:T(8,128)(2,1)S(1)}, u32[]{:S(2)}, u32[]{:S(2)}) collective-permute-start(bf16[2,64,512]{2,1,0:T(8,128)(2,1)S(1)} %get-tuple-element.22.here_ref), channel_id=1, source_target_pairs={{0,252},{4,0},{8,4},{12,8},{16,12},{20,16},{24,20},{28,24},{32,28}... | collective-permute-start | bytes 393224 | tf_op jit(solution)/shard_map/ppermute | solution.py:172
  19.3 7.6 %collective-permute-start.3 = (bf16[2,64,512]{2,1,0:T(8,128)(2,1)S(1)}, bf16[2,64,512]{2,1,0:T(8,128)(2,1)S(1)}, u32[]{:S(2)}, u32[]{:S(2)}) collective-permute-start(bf16[2,64,512]{2,1,0:T(8,128)(2,1)S(1)} %get-tuple-element.22.here_ref), channel_id=1, source_target_pairs={{0,248},{4,252},{8,0},{12,4},{16,8},{20,12},{24,16},{28,20},{32,24... | collective-permute-start | bytes 393224 | tf_op jit(solution)/shard_map/ppermute | solution.py:172
  29.0 2.7 %collective-permute-start.8 = (bf16[2,64,384]{2,1,0:T(8,128)(2,1)S(1)}, bf16[2,64,384]{2,1,0:T(8,128)(2,1)S(1)}, u32[]{:S(2)}, u32[]{:S(2)}) collective-permute-start(bf16[2,64,384]{2,1,0:T(8,128)(2,1)S(1)} %get-tuple-element.26), channel_id=1, source_target_pairs={{0,1},{1,0},{2,3},{3,2},{4,5},{5,4},{6,7},{7,6},{8,9},{9,8},{10,11... | collective-permute-start | bytes 294920 | tf_op jit(solution)/shard_map/ppermute | solution.py:177
  30.8 4.0 %collective-permute-start.7 = (bf16[2,64,384]{2,1,0:T(8,128)(2,1)S(1)}, bf16[2,64,384]{2,1,0:T(8,128)(2,1)S(1)}, u32[]{:S(2)}, u32[]{:S(2)}) collective-permute-start(bf16[2,64,384]{2,1,0:T(8,128)(2,1)S(1)} %get-tuple-element.24), channel_id=1, source_target_pairs={{0,1},{1,0},{2,3},{3,2},{4,5},{5,4},{6,7},{7,6},{8,9},{9,8},{10,11... | collective-permute-start | bytes 294920 | tf_op jit(solution)/shard_map/ppermute | solution.py:177
  31.8 5.6 %collective-permute-start.9 = (bf16[2,64,384]{2,1,0:T(8,128)(2,1)S(1)}, bf16[2,64,384]{2,1,0:T(8,128)(2,1)S(1)}, u32[]{:S(2)}, u32[]{:S(2)}) collective-permute-start(bf16[2,64,384]{2,1,0:T(8,128)(2,1)S(1)} %add_convert_fusion.1), channel_id=1, source_target_pairs={{0,2},{1,3},{2,0},{3,1},{4,6},{5,7},{6,4},{7,5},{8,10},{9,11},{10,... | collective-permute-start | bytes 294920 | tf_op jit(solution)/shard_map/ppermute | solution.py:177

commit v3 on v2

--- a/solution.py
+++ b/solution.py
@@ -40,18 +40,25 @@
     ).astype(F32).astype(BF16)
 
 
-def to_distance(weights):
-    count = weights.shape[0]
+def flip(rows):
+    down = lax.broadcasted_iota(jnp.int32, (BLK, BLK), 0)
+    along = lax.broadcasted_iota(jnp.int32, (BLK, BLK), 1)
+    swap = (down + along == BLK - 1).astype(F32).astype(BF16)
+    return dot(swap, rows).astype(BF16)
+
+
+def to_window(table):
+    count = table.shape[0]
     moved = jnp.concatenate(
         [
-            pltpu.roll(weights[at : at + 8], BLK - 8 - at % BLK, 1) if at % BLK != BLK - 8 else weights[at : at + 8]
+            pltpu.roll(table[at : at + 8], SPAN - at % BLK, 1) if at % BLK else table[at : at + 8]
             for at in range(0, count, 8)
         ],
         axis=0,
     )
-    rest = 7 - lax.broadcasted_iota(jnp.int32, moved.shape, 0) % 8
+    rest = lax.broadcasted_iota(jnp.int32, moved.shape, 0) % 8
     for bit in (4, 2, 1):
-        moved = jnp.where(rest & bit != 0, pltpu.roll(moved, bit, 1), moved)
+        moved = jnp.where(rest & bit != 0, pltpu.roll(moved, SPAN - bit, 1), moved)
     return moved
 
 
@@ -88,28 +95,23 @@
     query_ref[...] = project(query_weight_ref)
 
 
-def table_kernel(rel_key_ref, bucket_ref, gain_ref, table_ref, gain_out_ref):
+def gain_kernel(gain_ref, gain_out_ref):
+    gain_out_ref[...] = gain_ref[...]
+
+
+def position_kernel(query_ref, rel_key_ref, bucket_ref, flipped_ref, place_ref):
     hot = one_hot(bucket_ref, rel_key_ref.shape[0])
-    table_ref[...] = dot(rel_key_ref[...], hot, TN).astype(BF16)
-    gain_out_ref[...] = gain_ref[...]
-
-
-def position_kernel(query_ref, table_ref, place_ref):
-    query = query_ref[...]
-    sequences = query.shape[0] // BLK
-    for seq in range(sequences):
-        stacked = by_head(query[seq * BLK : (seq + 1) * BLK])
-        table = dot(stacked, table_ref[...])
-        for head in range(2):
-            part = table[head * BLK : (head + 1) * BLK]
-            place_ref[seq, head * BLK : (head + 1) * BLK, :] = pltpu.roll(
-                part, SPAN - (BLK - 1), 1, stride=1, stride_axis=0
-            )
+    by_distance = dot(rel_key_ref[...], hot, TN).astype(BF16)
+    for seq in range(place_ref.shape[0]):
+        rows = slice(seq * BLK, (seq + 1) * BLK)
+        flipped = flip(query_ref[rows, :])
+        flipped_ref[rows, :] = flipped
+        place_ref[seq] = to_window(dot(by_head(flipped), by_distance))
 
 
 def attend_kernel(
-    query_ref, place_ref, up2_ref, up1_ref, here_ref, low1_ref, low2_ref, bias_ref, rel_value_ref,
-    bucket_ref, out_weight_ref, own_ref, first_ref, second_ref, third_ref,
+    query_ref, place_ref, here_ref, up1_ref, up2_ref, low2_ref, low1_ref, bias_ref, rel_value_ref,
+    bucket_ref, out_weight_ref, context_ref, corner_ref,
 ):
     sequences = query_ref.shape[0] // BLK
     parts = (low2_ref, low1_ref, here_ref, up1_ref, up2_ref)
@@ -139,19 +141,36 @@
         total = jnp.sum(expo, axis=-1, keepdims=True)
         weights = expo.astype(BF16)
         rounded = weights.astype(F32)
-        spread = to_distance(rounded).astype(BF16)
+        spread = jnp.concatenate(
+            [
+                pltpu.roll(rounded[head * BLK : (head + 1) * BLK], 0, 1, stride=1, stride_axis=0)
+                for head in range(2)
+            ],
+            axis=0,
+        ).astype(BF16)
         bucketed = dot(spread, hot, NT).astype(BF16)
         summed = dot(weights, values) + dot(bucketed, rel_value_ref[...])
         summed = summed / total
         side = lax.broadcasted_iota(jnp.int32, (BLK, 2 * VAL), 1)
-        contexts.append(jnp.where(side < VAL, summed[:BLK], summed[BLK:]).astype(BF16))
+        contexts.append(flip(jnp.where(side < VAL, summed[:BLK], summed[BLK:]).astype(BF16)))
     context = jnp.concatenate(contexts, axis=0)
+    context_ref[...] = context
+    project_out(context, out_weight_ref, ((3, corner_ref),))
+
+
+def project_out(context, out_weight_ref, targets):
     me = lax.axis_index("ch")
-    width = own_ref.shape[2]
-    for order, target in enumerate((own_ref, first_ref, second_ref, third_ref)):
+    for order, target in targets:
+        sequences, rows, width = target.shape
         at = pl.multiple_of((me ^ order) * width, width)
         partial_value = dot(context, out_weight_ref[:, pl.ds(at, width)]).astype(BF16)
-        target[...] = partial_value.reshape(sequences, BLK, width)
+        target[...] = partial_value.reshape(sequences, rows, width)
+
+
+def output_kernel(context_ref, out_weight_ref, own_ref, beside_ref, across_ref):
+    project_out(
+        context_ref[...], out_weight_ref, ((2, across_ref), (1, beside_ref), (0, own_ref))
+    )
 
 
 def call(kernel, outs, cost):
@@ -186,11 +205,10 @@
     bucket = jnp.pad(bucket_of, (0, SPAN - bucket_of.shape[0]), constant_values=-1).reshape(1, SPAN)
     packed_width = w_key.shape[1] + w_value.shape[1]
     across = crossed(tokens, "ch", 2)
-    beside = crossed(tokens, "ch", 1)
-    table, gain = call(
-        table_kernel, [shape(w_key.shape[1], SPAN), shape(*gain.shape)], 20 << 30
-    )(rel_key, bucket, gain)
-    across, table, gain = lax.optimization_barrier((across, table, gain))
+    gain = call(gain_kernel, shape(*gain.shape), 20 << 30)(gain)
+    beside, gain = lax.optimization_barrier((tokens, gain))
+    beside = crossed(beside, "ch", 1)
+    across, gain = lax.optimization_barrier((across, gain))
     corner = crossed(across, "ch", 1)
     packed, query = call(
         project_kernel,
@@ -201,12 +219,15 @@
     low1 = shifted(packed, "seq", 1)
     up1 = shifted(packed, "seq", -1)
     up2 = shifted(packed, "seq", -2)
-    place = call(
-        position_kernel, shape(sequences, 2 * BLK, SPAN, dtype=F32), 300 << 20
-    )(query, table)
-    own, beside, across, corner = call(
-        attend_kernel, [shape(sequences, rows, width)] * 4, 1 << 30
-    )(query, place, up2, up1, packed, low1, low2, bias, rel_value, bucket, w_out)
+    flipped, place = call(
+        position_kernel, [shape(*query.shape), shape(sequences, 2 * BLK, SPAN, dtype=F32)], 300 << 20
+    )(query, rel_key, bucket)
+    context, corner = call(
+        attend_kernel, [shape(sequences * rows, w_out.shape[0]), shape(sequences, rows, width)], 1 << 30
+    )(flipped, place, packed, up1, up2, low2, low1, bias, rel_value, bucket, w_out)
+    own, beside, across = call(output_kernel, [shape(sequences, rows, width)] * 3, 300 << 20)(
+        context, w_out
+    )
     pair = (across.astype(F32) + crossed(corner, "ch", 1).astype(F32)).astype(BF16)
     beside = crossed(beside, "ch", 1)
     pair = crossed(pair, "ch", 2)

time: 38.3 us -> 36.3 us (0.948)
  waiting for transfers between devices: 12.1 us -> 7.35 us
  starting transfers between devices: 19.5 us -> 22.5 us
  local copies, waits for them, and re-layouts: 2.1 us -> 1.59 us
    ppermute x6, waiting for transfers between devices: 7.06 us -> 4.34 us  [crossed(): return lax.ppermute(value, axis, [(at, at ^ flip) for at in range(count)])]
    ppermute x6, starting transfers between devices: 10.1 us -> 12.4 us  [crossed(): return lax.ppermute(value, axis, [(at, at ^ flip) for at in range(count)])]
    ppermute x4, waiting for transfers between devices: 5.07 us -> 3.01 us  [shifted(): lax.ppermute(value, axis, [(at, (at + steps) % count) for at in range(cou...]
    ppermute x4, starting transfers between devices: 9.49 us -> 10.2 us  [shifted(): lax.ppermute(value, axis, [(at, (at + steps) % count) for at in range(cou...]
    pad x1, local copies, waits for them, and re-layouts: 0.68 us -> 0.01 us  [body(): jnp.pad(bucket_of, (0, SPAN - bucket_of.shape[0]), constant_values=-1)]
    pallas_call x3 -> x4, Pallas kernels: 2.65 us -> 2.96 us  [the longest x1 1.73 us: body(): call(attend_kernel, [shape(sequences * rows, w_out.shape[0]), shape(seque...]
    unnamed x16 -> x18, local copies, waits for them, and re-layouts: 0.72 us -> 0.88 us
  transfers between devices with their start and end apart: 10 -> 10, of which waited for: 7 -> 5; matrix products, arithmetic and copies ran while one was open for 4% -> 2% of each run, Pallas kernels for 1% -> 3%
where the time goes in v3:
time: 36.3 us; the launch traced here: 36.2 us
  starting transfers between devices  22.5 us (62%)
  waiting for transfers between devices  7.35 us (20%)
  Pallas kernels  3.83 us (11%)
  local copies, waits for them, and re-layouts  1.59 us (4%)
  other arithmetic  0.72 us (2%)
    ppermute x6, starting transfers between devices, crossed(): return lax.ppermute(value, axis, [(at, at ^ flip) for at in range(count)])  12.4 us
    ppermute x4, starting transfers between devices, shifted(): lax.ppermute(value, axis, [(at, (at + steps) % count) for at in range(cou...  10.2 us
    ppermute x6, waiting for transfers between devices, crossed(): return lax.ppermute(value, axis, [(at, at ^ flip) for at in range(count)])  4.34 us
    ppermute x4, waiting for transfers between devices, shifted(): lax.ppermute(value, axis, [(at, (at + steps) % count) for at in range(cou...  3.01 us
    pallas_call x1, Pallas kernels, body(): call(attend_kernel, [shape(sequences * rows, w_out.shape[0]), shape(seque...  1.73 us
    unnamed x18, local copies, waits for them, and re-layouts  0.88 us
    pallas_call x1, Pallas kernels, body(): call(position_kernel, [shape(*query.shape), shape(sequences, 2 * BLK, SPA...  0.88 us
    pallas_call x1, Pallas kernels, body(): call(project_kernel, [shape(sequences, rows, packed_width), shape(sequenc...  0.87 us
  transfers between devices with their start and end apart: 10, of which 5 were waited for; matrix products, arithmetic and copies ran while one was open for 2% of the time, Pallas kernels for 3%

profile of v3, /device:TPU:1, one launch (start us, length us, event | category | flops | bytes accessed | tf_op | source)
XLA Modules:
  0.0 36.2 jit_solution(3031719104858395304)
XLA Ops:
  0.0 3.7 %collective-permute-start.1 = (bf16[2,64,384]{2,1,0:T(8,128)(2,1)}, bf16[2,64,384]{2,1,0:T(8,128)(2,1)S(1)}, u32[]{:S(2)}, u32[]{:S(2)}) collective-permute-start(bf16[2,64,384]{2,1,0:T(8,128)(2,1)} %own_ref.1), channel_id=1, source_target_pairs={{0,2},{1,3},{2,0},{3,1},{4,6},{5,7},{6,4},{7,5},{8,10},{9,11},{10,... | collective-permute-start | bytes 294920 | tf_op jit(solution)/shard_map/ppermute | solution.py:196
  3.7 0.7 %reshape.9.gain_ref = bf16[1,1536]{1,0:T(2,128)(2,1)S(1)} reshape(bf16[1536]{0:T(1024)(128)(2,1)} %param.11) | data formatting | bytes 6144 | tf_op jit(solution)/shard_map/reshape | solution.py:203
  4.4 0.0 copy-start.2
  4.5 0.0 copy-start.3
  4.5 0.8 %copy-done.4 = bf16[2,64,384]{2,1,0:T(8,128)(2,1)S(1)} copy-done((bf16[2,64,384]{2,1,0:T(8,128)(2,1)S(1)}, bf16[2,64,384]{2,1,0:T(8,128)(2,1)}, u32[]{:S(2)}) %copy-start.4) | copy-done | bytes 98328
  5.3 1.0 %collective-permute-start = (bf16[2,64,384]{2,1,0:T(8,128)(2,1)S(1)}, bf16[2,64,384]{2,1,0:T(8,128)(2,1)S(1)}, u32[]{:S(2)}, u32[]{:S(2)}) collective-permute-start(bf16[2,64,384]{2,1,0:T(8,128)(2,1)S(1)} %copy-done.4), channel_id=1, source_target_pairs={{0,1},{1,0},{2,3},{3,2},{4,5},{5,4},{6,7},{7,6},{8,9},{9,8},{10,11... | collective-permute-start | bytes 294920 | tf_op jit(solution)/shard_map/ppermute | solution.py:196
  6.3 3.3 %collective-permute-start.2 = (bf16[2,64,384]{2,1,0:T(8,128)(2,1)S(1)}, bf16[2,64,384]{2,1,0:T(8,128)(2,1)S(1)}, u32[]{:S(2)}, u32[]{:S(2)}) collective-permute-start(bf16[2,64,384]{2,1,0:T(8,128)(2,1)S(1)} %collective-permute-done.1.across_ref), channel_id=1, source_target_pairs={{0,1},{1,0},{2,3},{3,2},{4,5},{5,4},{6,7},{7,6},{8,9},{9,8},{10,11... | collective-permute-start | bytes 294920 | tf_op jit(solution)/shard_map/ppermute | solution.py:196
  9.6 0.9 %collective-permute-done.2.corner_ref = bf16[2,64,384]{2,1,0:T(8,128)(2,1)S(1)} collective-permute-done((bf16[2,64,384]{2,1,0:T(8,128)(2,1)S(1)}, bf16[2,64,384]{2,1,0:T(8,128)(2,1)S(1)}, u32[]{:S(2)}, u32[]{:S(2)}) %collective-permute-start.2) | collective-permute-done | bytes 98336 | tf_op jit(solution)/shard_map/ppermute | solution.py:196
  10.5 0.9 %shard_map.101 = (bf16[2,64,512]{2,1,0:T(8,128)(2,1)S(1)}, bf16[128,128]{1,0:T(8,128)(2,1)S(1)}) custom-call(bf16[2,64,384]{2,1,0:T(8,128)(2,1)S(1)} %copy-done.4, bf16[2,64,384]{2,1,0:T(8,128)(2,1)S(1)} %collective-permute-done.beside_ref, bf16[2,64,384]{2,1,0:T(8,128)(2,1)S(1)} %collective-permute-done.1.across_ref, ...), custom_call_target="tpu_custom_call" | custom-call | flops 314572800 | bytes 1048576 | tf_op jit(solution)/shard_map/pallas_call | solution.py:213
  11.4 0.1 collective-permute-start.6
  11.5 1.9 %collective-permute-start.5 = (bf16[2,64,512]{2,1,0:T(8,128)(2,1)S(1)}, bf16[2,64,512]{2,1,0:T(8,128)(2,1)S(1)}, u32[]{:S(2)}, u32[]{:S(2)}) collective-permute-start(bf16[2,64,512]{2,1,0:T(8,128)(2,1)S(1)} %get-tuple-element.25.here_ref), channel_id=1, source_target_pairs={{0,8},{4,12},{8,16},{12,20},{16,24},{20,28},{24,32},{28,36},{32,40... | collective-permute-start | bytes 393224 | tf_op jit(solution)/shard_map/ppermute | solution.py:191
  13.4 6.3 %collective-permute-start.4 = (bf16[2,64,512]{2,1,0:T(8,128)(2,1)S(1)}, bf16[2,64,512]{2,1,0:T(8,128)(2,1)S(1)}, u32[]{:S(2)}, u32[]{:S(2)}) collective-permute-start(bf16[2,64,512]{2,1,0:T(8,128)(2,1)S(1)} %get-tuple-element.25.here_ref), channel_id=1, source_target_pairs={{0,248},{4,252},{8,0},{12,4},{16,8},{20,12},{24,16},{28,20},{32,24... | collective-permute-start | bytes 393224 | tf_op jit(solution)/shard_map/ppermute | solution.py:191
  19.7 1.9 %collective-permute-start.3 = (bf16[2,64,512]{2,1,0:T(8,128)(2,1)S(1)}, bf16[2,64,512]{2,1,0:T(8,128)(2,1)S(1)}, u32[]{:S(2)}, u32[]{:S(2)}) collective-permute-start(bf16[2,64,512]{2,1,0:T(8,128)(2,1)S(1)} %get-tuple-element.25.here_ref), channel_id=1, source_target_pairs={{0,252},{4,0},{8,4},{12,8},{16,12},{20,16},{24,20},{28,24},{32,28}... | collective-permute-start | bytes 393224 | tf_op jit(solution)/shard_map/ppermute | solution.py:191
  21.6 0.9 %shard_map.102 = (bf16[128,128]{1,0:T(8,128)(2,1)S(1)}, f32[2,128,384]{2,1,0:T(8,128)S(1)}) custom-call(bf16[128,128]{1,0:T(8,128)(2,1)S(1)} %get-tuple-element.22.query_ref, bf16[32,128]{1,0:T(8,128)(2,1)S(1)} %copy-done.6, s32[1,384]{1,0:T(1,128)S(1)} %reshape.10.bucket_ref), custom_call_target="tpu_custom_call" | custom-call | flops 314572800 | bytes 1048576 | tf_op jit(solution)/shard_map/pallas_call | solution.py:222
  22.5 1.3 %collective-permute-done.6.low1_ref = bf16[2,64,512]{2,1,0:T(8,128)(2,1)S(1)} collective-permute-done((bf16[2,64,512]{2,1,0:T(8,128)(2,1)S(1)}, bf16[2,64,512]{2,1,0:T(8,128)(2,1)S(1)}, u32[]{:S(2)}, u32[]{:S(2)}) %collective-permute-start.6) | collective-permute-done | bytes 131104 | tf_op jit(solution)/shard_map/ppermute | solution.py:191
  23.8 1.7 %collective-permute-done.5.low2_ref = bf16[2,64,512]{2,1,0:T(8,128)(2,1)S(1)} collective-permute-done((bf16[2,64,512]{2,1,0:T(8,128)(2,1)S(1)}, bf16[2,64,512]{2,1,0:T(8,128)(2,1)S(1)}, u32[]{:S(2)}, u32[]{:S(2)}) %collective-permute-start.5) | collective-permute-done | bytes 131104 | tf_op jit(solution)/shard_map/ppermute | solution.py:191
  25.6 1.7 %shard_map.103 = (bf16[128,384]{1,0:T(8,128)(2,1)S(1)}, bf16[2,64,384]{2,1,0:T(8,128)(2,1)S(1)}) custom-call(bf16[128,128]{1,0:T(8,128)(2,1)S(1)} %get-tuple-element.23.query_ref, f32[2,128,384]{2,1,0:T(8,128)S(1)} %get-tuple-element.24.place_ref, bf16[2,64,512]{2,1,0:T(8,128)(2,1)S(1)} %get-tuple-element.25.here_ref, ...), custom_call_target="tpu_custom_call" | custom-call | flops 1073741824 | bytes 1048576 | tf_op jit(solution)/shard_map/pallas_call | solution.py:225
  27.3 1.6 %collective-permute-start.8 = (bf16[2,64,384]{2,1,0:T(8,128)(2,1)S(1)}, bf16[2,64,384]{2,1,0:T(8,128)(2,1)S(1)}, u32[]{:S(2)}, u32[]{:S(2)}) collective-permute-start(bf16[2,64,384]{2,1,0:T(8,128)(2,1)S(1)} %get-tuple-element.30), channel_id=1, source_target_pairs={{0,1},{1,0},{2,3},{3,2},{4,5},{5,4},{6,7},{7,6},{8,9},{9,8},{10,11... | collective-permute-start | bytes 294920 | tf_op jit(solution)/shard_map/ppermute | solution.py:196
  28.9 0.3 shard_map.104
  29.2 0.1 collective-permute-start.7
  29.3 0.5 %collective-permute-done.8 = bf16[2,64,384]{2,1,0:T(8,128)(2,1)S(1)} collective-permute-done((bf16[2,64,384]{2,1,0:T(8,128)(2,1)S(1)}, bf16[2,64,384]{2,1,0:T(8,128)(2,1)S(1)}, u32[]{:S(2)}, u32[]{:S(2)}) %collective-permute-start.8) | collective-permute-done | bytes 98336 | tf_op jit(solution)/shard_map/ppermute | solution.py:196
  29.8 2.7 %collective-permute-start.9 = (bf16[2,64,384]{2,1,0:T(8,128)(2,1)S(1)}, bf16[2,64,384]{2,1,0:T(8,128)(2,1)S(1)}, u32[]{:S(2)}, u32[]{:S(2)}) collective-permute-start(bf16[2,64,384]{2,1,0:T(8,128)(2,1)S(1)} %add_convert_fusion.1), channel_id=1, source_target_pairs={{0,2},{1,3},{2,0},{3,1},{4,6},{5,7},{6,4},{7,5},{8,10},{9,11},{10,... | collective-permute-start | bytes 294920 | tf_op jit(solution)/shard_map/ppermute | solution.py:196
  32.5 2.9 %collective-permute-done.9 = bf16[2,64,384]{2,1,0:T(8,128)(2,1)S(1)} collective-permute-done((bf16[2,64,384]{2,1,0:T(8,128)(2,1)S(1)}, bf16[2,64,384]{2,1,0:T(8,128)(2,1)S(1)}, u32[]{:S(2)}, u32[]{:S(2)}) %collective-permute-start.9) | collective-permute-done | bytes 98336 | tf_op jit(solution)/shard_map/ppermute | solution.py:196
  35.5 0.7 %add_convert_fusion = bf16[2,64,384]{2,1,0:T(8,128)(2,1)} fusion(bf16[2,64,384]{2,1,0:T(8,128)(2,1)S(1)} %collective-permute-done.9, bf16[2,64,384]{2,1,0:T(8,128)(2,1)S(1)} %collective-permute-done.7, bf16[2,64,384]{2,1,0:T(8,128)(2,1)S(1)} %get-tuple-element.27, bf16[2,64,384]{2,1,0:T(8,128)(2,1)S(1)} %copy-done.4), kind=kLoop, calls=%fused_computation | loop fusion | flops 393216 | bytes 491520 | tf_op jit(solution)/shard_map/convert_element_type | solution.py:235
  (24 shorter events, 0.1 us)
Async XLA Ops:
  0.0 6.3 %collective-permute-start.1 = (bf16[2,64,384]{2,1,0:T(8,128)(2,1)}, bf16[2,64,384]{2,1,0:T(8,128)(2,1)S(1)}, u32[]{:S(2)}, u32[]{:S(2)}) collective-permute-start(bf16[2,64,384]{2,1,0:T(8,128)(2,1)} %own_ref.1), channel_id=1, source_target_pairs={{0,2},{1,3},{2,0},{3,1},{4,6},{5,7},{6,4},{7,5},{8,10},{9,11},{10,... | collective-permute-start | bytes 294920 | tf_op jit(solution)/shard_map/ppermute | solution.py:196
  4.4 0.9 %copy-start.4 = (bf16[2,64,384]{2,1,0:T(8,128)(2,1)S(1)}, bf16[2,64,384]{2,1,0:T(8,128)(2,1)}, u32[]{:S(2)}) copy-start(bf16[2,64,384]{2,1,0:T(8,128)(2,1)} %own_ref.1) | copy-start | bytes 294916
  4.4 6.1 %copy-start.1 = (bf16[1536,384]{1,0:T(8,128)(2,1)S(1)}, bf16[1536,384]{1,0:T(8,128)(2,1)}, u32[]{:S(2)}) copy-start(bf16[1536,384]{1,0:T(8,128)(2,1)} %value_ref.1) | copy-start | bytes 3538948
  4.4 6.1 %copy-start.2 = (bf16[1536,128]{1,0:T(8,128)(2,1)S(1)}, bf16[1536,128]{1,0:T(8,128)(2,1)}, u32[]{:S(2)}) copy-start(bf16[1536,128]{1,0:T(8,128)(2,1)} %key_ref.1) | copy-start | bytes 1179652
  4.5 6.1 %copy-start.3 = (bf16[1536,128]{1,0:T(8,128)(2,1)S(1)}, bf16[1536,128]{1,0:T(8,128)(2,1)}, u32[]{:S(2)}) copy-start(bf16[1536,128]{1,0:T(8,128)(2,1)} %query_weight_ref.1) | copy-start | bytes 1179652
  5.3 16.3 %copy-start.8 = (s32[383]{0:T(512)S(1)}, s32[383]{0:T(512)}, u32[]{:S(2)}) copy-start(s32[383]{0:T(512)} %param.19) | copy-start | bytes 4600
  5.3 16.3 %copy-start.6 = (bf16[32,128]{1,0:T(8,128)(2,1)S(1)}, bf16[32,128]{1,0:T(8,128)(2,1)}, u32[]{:S(2)}) copy-start(bf16[32,128]{1,0:T(8,128)(2,1)} %rel_key_ref.1) | copy-start | bytes 24580
  5.3 4.2 %collective-permute-start = (bf16[2,64,384]{2,1,0:T(8,128)(2,1)S(1)}, bf16[2,64,384]{2,1,0:T(8,128)(2,1)S(1)}, u32[]{:S(2)}, u32[]{:S(2)}) collective-permute-start(bf16[2,64,384]{2,1,0:T(8,128)(2,1)S(1)} %copy-done.4), channel_id=1, source_target_pairs={{0,1},{1,0},{2,3},{3,2},{4,5},{5,4},{6,7},{7,6},{8,9},{9,8},{10,11... | collective-permute-start | bytes 294920 | tf_op jit(solution)/shard_map/ppermute | solution.py:196
  6.3 4.2 %collective-permute-start.2 = (bf16[2,64,384]{2,1,0:T(8,128)(2,1)S(1)}, bf16[2,64,384]{2,1,0:T(8,128)(2,1)S(1)}, u32[]{:S(2)}, u32[]{:S(2)}) collective-permute-start(bf16[2,64,384]{2,1,0:T(8,128)(2,1)S(1)} %collective-permute-done.1.across_ref), channel_id=1, source_target_pairs={{0,1},{1,0},{2,3},{3,2},{4,5},{5,4},{6,7},{7,6},{8,9},{9,8},{10,11... | collective-permute-start | bytes 294920 | tf_op jit(solution)/shard_map/ppermute | solution.py:196
  10.5 15.0 %copy-start.5 = (bf16[32,384]{1,0:T(8,128)(2,1)S(1)}, bf16[32,384]{1,0:T(8,128)(2,1)}, u32[]{:S(2)}) copy-start(bf16[32,384]{1,0:T(8,128)(2,1)} %rel_value_ref.1) | copy-start | bytes 73732
  11.4 14.1 %copy-start = (bf16[384,1536]{1,0:T(8,128)(2,1)S(1)}, bf16[384,1536]{1,0:T(8,128)(2,1)}, u32[]{:S(2)}) copy-start(bf16[384,1536]{1,0:T(8,128)(2,1)} %out_weight_ref.3) | copy-start | bytes 3538948
  11.4 14.1 %copy-start.7 = (bf16[128]{0:T(256)(128)(2,1)S(1)}, bf16[128]{0:T(256)(128)(2,1)}, u32[]{:S(2)}) copy-start(bf16[128]{0:T(256)(128)(2,1)} %param.16) | copy-start | bytes 772
  11.4 12.4 %collective-permute-start.6 = (bf16[2,64,512]{2,1,0:T(8,128)(2,1)S(1)}, bf16[2,64,512]{2,1,0:T(8,128)(2,1)S(1)}, u32[]{:S(2)}, u32[]{:S(2)}) collective-permute-start(bf16[2,64,512]{2,1,0:T(8,128)(2,1)S(1)} %get-tuple-element.25.here_ref), channel_id=1, source_target_pairs={{0,4},{4,8},{8,12},{12,16},{16,20},{20,24},{24,28},{28,32},{32,36}... | collective-permute-start | bytes 393224 | tf_op jit(solution)/shard_map/ppermute | solution.py:191
  11.5 14.0 %collective-permute-start.5 = (bf16[2,64,512]{2,1,0:T(8,128)(2,1)S(1)}, bf16[2,64,512]{2,1,0:T(8,128)(2,1)S(1)}, u32[]{:S(2)}, u32[]{:S(2)}) collective-permute-start(bf16[2,64,512]{2,1,0:T(8,128)(2,1)S(1)} %get-tuple-element.25.here_ref), channel_id=1, source_target_pairs={{0,8},{4,12},{8,16},{12,20},{16,24},{20,28},{24,32},{28,36},{32,40... | collective-permute-start | bytes 393224 | tf_op jit(solution)/shard_map/ppermute | solution.py:191
  13.4 12.1 %collective-permute-start.4 = (bf16[2,64,512]{2,1,0:T(8,128)(2,1)S(1)}, bf16[2,64,512]{2,1,0:T(8,128)(2,1)S(1)}, u32[]{:S(2)}, u32[]{:S(2)}) collective-permute-start(bf16[2,64,512]{2,1,0:T(8,128)(2,1)S(1)} %get-tuple-element.25.here_ref), channel_id=1, source_target_pairs={{0,248},{4,252},{8,0},{12,4},{16,8},{20,12},{24,16},{28,20},{32,24... | collective-permute-start | bytes 393224 | tf_op jit(solution)/shard_map/ppermute | solution.py:191
  19.7 5.8 %collective-permute-start.3 = (bf16[2,64,512]{2,1,0:T(8,128)(2,1)S(1)}, bf16[2,64,512]{2,1,0:T(8,128)(2,1)S(1)}, u32[]{:S(2)}, u32[]{:S(2)}) collective-permute-start(bf16[2,64,512]{2,1,0:T(8,128)(2,1)S(1)} %get-tuple-element.25.here_ref), channel_id=1, source_target_pairs={{0,252},{4,0},{8,4},{12,8},{16,12},{20,16},{24,20},{28,24},{32,28}... | collective-permute-start | bytes 393224 | tf_op jit(solution)/shard_map/ppermute | solution.py:191
  27.3 2.5 %collective-permute-start.8 = (bf16[2,64,384]{2,1,0:T(8,128)(2,1)S(1)}, bf16[2,64,384]{2,1,0:T(8,128)(2,1)S(1)}, u32[]{:S(2)}, u32[]{:S(2)}) collective-permute-start(bf16[2,64,384]{2,1,0:T(8,128)(2,1)S(1)} %get-tuple-element.30), channel_id=1, source_target_pairs={{0,1},{1,0},{2,3},{3,2},{4,5},{5,4},{6,7},{7,6},{8,9},{9,8},{10,11... | collective-permute-start | bytes 294920 | tf_op jit(solution)/shard_map/ppermute | solution.py:196
  29.2 3.3 %collective-permute-start.7 = (bf16[2,64,384]{2,1,0:T(8,128)(2,1)S(1)}, bf16[2,64,384]{2,1,0:T(8,128)(2,1)S(1)}, u32[]{:S(2)}, u32[]{:S(2)}) collective-permute-start(bf16[2,64,384]{2,1,0:T(8,128)(2,1)S(1)} %get-tuple-element.28), channel_id=1, source_target_pairs={{0,1},{1,0},{2,3},{3,2},{4,5},{5,4},{6,7},{7,6},{8,9},{9,8},{10,11... | collective-permute-start | bytes 294920 | tf_op jit(solution)/shard_map/ppermute | solution.py:196
  29.8 5.6 %collective-permute-start.9 = (bf16[2,64,384]{2,1,0:T(8,128)(2,1)S(1)}, bf16[2,64,384]{2,1,0:T(8,128)(2,1)S(1)}, u32[]{:S(2)}, u32[]{:S(2)}) collective-permute-start(bf16[2,64,384]{2,1,0:T(8,128)(2,1)S(1)} %add_convert_fusion.1), channel_id=1, source_target_pairs={{0,2},{1,3},{2,0},{3,1},{4,6},{5,7},{6,4},{7,5},{8,10},{9,11},{10,... | collective-permute-start | bytes 294920 | tf_op jit(solution)/shard_map/ppermute | solution.py:196
